TPU v7x, 1024 devices: a whole 8x8x8 slice. The times are simulated.
1024 devices in a mesh: col: 64 (over x, z), row: 8 (over y), lev: 2 (over core).
Axes of the slice: x: 8, y: 8, z: 8, core: 2. Of those that a mesh axis runs over, the one named last changes fastest.
Arguments:
- state: float32 [2, 8, 512, 32768], P(None, 'lev', 'row', 'col'), may hold values from -6 to 6
- atm_flux: bfloat16 [8, 2, 3072, 512], P('row', 'lev', 'col'), may hold values from -6 to 6
- intersection: int32 [8, 2, 3072, 2], P('row', 'lev', 'col'), may hold values from 0 to 63, all different within a row; in each aligned block of 48 rows (0 to 47, 48 to 95, ..., all dimensions but the last counted through in order) at most 3 rows name the same one
- weight_index: int32 [8, 2, 3072, 2], P('row', 'lev', 'col'), may hold values from 0 to 23
- target_row: int32 [8, 2, 3072, 2], P('row', 'lev', 'col'), may hold values from 0 to 63
- remap_weights: bfloat16 [24, 128, 512], replicated, may hold values from -0.5 to 0.5
- land_mask: int32 [512, 32768], P('row', 'col'), may hold values 0 or 1
- profiles: float32 [3, 8], P(None, 'lev'), may hold values from 0.2 to 1
Outputs:
- final_state: float32 [2, 8, 512, 32768], P(None, 'lev', 'row', 'col')
Inputs may be any that keep to these rules, and one draw needn't show every extreme that they name: `intersection`: the two partitions of one block differ; at most 3 of the blocks on one device name the same partition, and some device's blocks name one partition exactly 3 times.
All inputs are finite; a program needn't handle non-finite values. No bound on the sum of `land_mask` on one device may be relied on, other than what follows from the above.
Results may differ from a plain program's by a relative error of at most 0.00049.
Values may be sent and summed in bfloat16 or wider, within the bound.
A program may use at most 32 MiB of HBM per device.

v0:
```python
import jax
import jax.numpy as jnp
from jax import lax
from jax.sharding import PartitionSpec as P

STEPS = 4


DIFFUSE = 0.2
SPEED = 0.3
FORCE_STEP = 0.25


def extended(cells, sides, width):
    for axis, dim in sides:
        count = lax.axis_size(axis)
        ends = count - 1
        head = lax.slice_in_dim(cells, 0, width, axis=dim)
        tail = lax.slice_in_dim(cells, cells.shape[dim] - width, cells.shape[dim], axis=dim)
        cells = jnp.concatenate(
            [
                lax.ppermute(tail, axis, [(i, (i + 1) % count) for i in range(ends)]),
                cells,
                lax.ppermute(head, axis, [((i + 1) % count, i) for i in range(ends)]),
            ],
            axis=dim,
        )
    return cells


def advance(tracer, padded, east_speed, north_speed, source, wet):
    center = padded[..., 1:-1, 1:-1]
    east = padded[..., 1:-1, 2:]
    west = padded[..., 1:-1, :-2]
    north = padded[..., 2:, 1:-1]
    south = padded[..., :-2, 1:-1]
    fresh = center + DIFFUSE * (east + west + north + south - 4.0 * center)
    fresh = fresh - 0.5 * east_speed * (east - west) - 0.5 * north_speed * (north - south)
    fresh = fresh + FORCE_STEP * source
    return jnp.where(wet, fresh, tracer)


def coefficients(forcing, profiles):
    east_speed = SPEED * jnp.tanh(forcing[2])[None] * profiles[2][:, None, None]
    north_speed = SPEED * jnp.tanh(forcing[3])[None] * profiles[2][:, None, None]
    source = jnp.stack(
        [
            forcing[0][None] * profiles[0][:, None, None],
            forcing[1][None] * profiles[1][:, None, None],
        ]
    )
    return (east_speed, north_speed, source)


def remap_slots(slot_flux, slot_bins, remap_weights, lat_rows):
    blocks, cells, width = remap_weights.shape
    onehot = (slot_bins[:, None] == jnp.arange(lat_rows * blocks, dtype=jnp.int32)[None, :]).astype(
        jnp.bfloat16
    )
    grouped = lax.dot_general(
        onehot, slot_flux, (((0,), (0,)), ((), ())), preferred_element_type=jnp.float32
    )
    grouped = grouped.astype(jnp.bfloat16)
    rows = (
        grouped.reshape(lat_rows, blocks, 4, cells)
        .transpose(0, 2, 1, 3)
        .reshape(lat_rows * 4, blocks * cells)
    )
    part = jnp.dot(
        rows, remap_weights.reshape(blocks * cells, width), preferred_element_type=jnp.float32
    )
    return part.reshape(lat_rows, 4, width).transpose(1, 0, 2)


def local(
    state, atm_flux, intersection, weight_index, target_row, remap_weights, land_mask, profiles
):
    columns = lax.axis_size("col")
    blocks, cells, width = remap_weights.shape
    lat_rows = land_mask.shape[0]
    per_device = atm_flux.shape[2]
    pairs = 2 * per_device
    capacity = max(2, 4 * per_device // columns)
    slots = columns * capacity
    destination = intersection.reshape(pairs)
    pair_bins = (target_row * blocks + weight_index).reshape(pairs)
    dest_table = (destination[:, None] == jnp.arange(columns, dtype=jnp.int32)[None, :]).astype(
        jnp.int32
    )
    earlier = jnp.cumsum(dest_table, axis=0) - dest_table
    position = destination * capacity + jnp.sum(earlier * dest_table, axis=1)
    placing = position[None, :] == jnp.arange(slots, dtype=jnp.int32)[:, None]
    pair_flux = jnp.repeat(atm_flux.reshape(per_device, 4 * cells), 2, axis=0)
    send_flux = jnp.dot(
        placing.astype(jnp.bfloat16), pair_flux, preferred_element_type=jnp.float32
    ).astype(jnp.bfloat16)
    send_bins = jnp.sum(jnp.where(placing, pair_bins[None, :] + 1, 0), axis=1) - 1
    got_flux, got_bins = (
        lax.all_to_all(
            send_flux.reshape(columns, capacity, 4 * cells),
            "col",
            split_axis=0,
            concat_axis=0,
            tiled=True,
        ),
        lax.all_to_all(
            send_bins.reshape(columns, capacity), "col", split_axis=0, concat_axis=0, tiled=True
        ),
    )
    got_flux = got_flux.reshape(slots, 4 * cells)
    got_bins = got_bins.reshape(slots)
    forcing = lax.psum(remap_slots(got_flux, got_bins, remap_weights, lat_rows), "lev")
    wet = land_mask == 1
    east_speed, north_speed, source = coefficients(forcing, profiles)
    tracer = state
    for step in range(STEPS):
        padded = extended(tracer, (("col", 3), ("row", 2)), 1)
        tracer = advance(tracer, padded, east_speed, north_speed, source, wet)
    return tracer


def solution(mesh):
    in_specs = (
        P(None, "lev", "row", "col"),
        P("row", "lev", "col", None),
        P("row", "lev", "col", None),
        P("row", "lev", "col", None),
        P("row", "lev", "col", None),
        P(),
        P("row", "col"),
        P(None, "lev"),
    )
    out_specs = P(None, "lev", "row", "col")
    return jax.shard_map(local, mesh=mesh, in_specs=in_specs, out_specs=out_specs, check_vma=False)
```

profile of v0, /device:TPU:72, one launch (start us, length us, event | category | flops | bytes accessed | tf_op | source)
XLA Modules:
  0.0 199.5 jit_solution(356846302374892376)
XLA Ops:
  6.5 0.8 add_add_fusion
  7.6 0.8 copy.19
  9.0 0.7 sub.72
  9.8 22.7 %all-to-all-start = ((s32[64,1,3]{2,1,0:T(1,128)}), s32[64,1,3]{2,1,0:T(1,128)S(1)}, u32[]{:S(2)}, u32[]{:S(2)}) async-start(s32[64,1,3]{2,1,0:T(1,128)} %bitcast), calls=%async_computation | async-start | bytes 65536 | tf_op jit(solution)/shard_map/all_to_all | solution.py:106
  32.5 0.9 broadcast_in_dim.24
  33.6 0.8 reshape.77
  34.4 5.3 %all-to-all-done = s32[64,1,3]{2,1,0:T(1,128)S(1)} async-done(((s32[64,1,3]{2,1,0:T(1,128)}), s32[64,1,3]{2,1,0:T(1,128)S(1)}, u32[]{:S(2)}, u32[]{:S(2)}) %all-to-all-start) | async-done | bytes 800 | tf_op jit(solution)/shard_map/all_to_all | solution.py:106
  39.7 10.1 %all-to-all-start.1 = ((bf16[64,3,512]{2,1,0:T(4,128)(2,1)}), bf16[64,3,512]{2,1,0:T(4,128)(2,1)}, u32[]{:S(2)}, u32[]{:S(2)}) async-start(bf16[64,3,512]{2,1,0:T(4,128)(2,1)} %reshape.77), calls=%async_computation.1 | async-start | bytes 524288 | tf_op jit(solution)/shard_map/all_to_all | solution.py:99
  49.9 1.9 fusion.19
  51.8 3.4 %collective-permute-start.1 = (f32[2,4,64,1]{3,2,1,0:T(8,128)}, f32[2,4,64,1]{3,2,1,0:T(8,128)S(1)}, u32[]{:S(2)}, u32[]{:S(2)}) collective-permute-start(f32[2,4,64,1]{3,2,1,0:T(8,128)} %get-tuple-element.19), channel_id=1, source_target_pairs={{0,16},{16,32},{32,48},{48,64},{64,80},{80,96},{96,112},{112,128},... | collective-permute-start | bytes 6152 | tf_op jit(solution)/shard_map/ppermute | solution.py:22
  55.2 5.8 %collective-permute-start = (f32[2,4,64,1]{3,2,1,0:T(8,128)}, f32[2,4,64,1]{3,2,1,0:T(8,128)}, u32[]{:S(2)}, u32[]{:S(2)}) collective-permute-start(f32[2,4,64,1]{3,2,1,0:T(8,128)} %get-tuple-element.20), channel_id=1, source_target_pairs={{16,0},{32,16},{48,32},{64,48},{80,64},{96,80},{112,96},{128,112},... | collective-permute-start | bytes 6152 | tf_op jit(solution)/shard_map/ppermute | solution.py:24
  61.5 0.7 reduce.3
  62.4 1.8 reshape.78
  64.2 2.9 %convolution_convert_fusion = bf16[1536,512]{1,0:T(8,128)(2,1)} fusion(bf16[192,512]{1,0:T(8,128)(2,1)} %reshape.78, s32[192]{0:T(256)S(1)} %eq.55), kind=kOutput, calls=%fused_computation.2 | convolution fusion | flops 303071232 | bytes 1770240 | tf_op jit(solution)/shard_map/dot_general | solution.py:60
  67.0 3.5 %reshape.79 = bf16[64,24,4,128]{3,2,1,0:T(4,128)(2,1)} reshape(bf16[1536,512]{1,0:T(8,128)(2,1)} %convolution_convert_fusion) | data formatting | bytes 3145728 | tf_op jit(solution)/shard_map/reshape | solution.py:65
  70.5 3.2 %fusion.4 = f32[4,64,512]{2,1,0:T(8,128)} fusion(bf16[24,128,512]{2,1,0:T(8,128)(2,1)S(1)} %copy-done, bf16[64,24,4,128]{3,2,1,0:T(4,128)(2,1)} %reshape.79), kind=kOutput, calls=%fused_computation.5 | convolution fusion | flops 805306368 | bytes 5242880 | tf_op jit(solution)/shard_map/dot_general | solution.py:69
  73.7 0.9 broadcast_compare_fusion
  74.7 1.2 pad_maximum_fusion.43
  75.9 2.2 %collective-permute-start.2 = (f32[2,4,1,514]{3,2,1,0:T(1,128)S(1)}, f32[2,4,1,514]{3,2,1,0:T(1,128)S(1)}, u32[]{:S(2)}, u32[]{:S(2)}) collective-permute-start(f32[2,4,1,514]{3,2,1,0:T(1,128)S(1)} %get-tuple-element.11), channel_id=1, source_target_pairs={{2,0},{4,2},{6,4},{8,6},{10,8},{12,10},{14,12},{3,1},{5,3},{7,5},{... | collective-permute-start | bytes 49352 | tf_op jit(solution)/shard_map/ppermute | solution.py:24
  78.1 3.6 %collective-permute-start.3 = (f32[2,4,1,514]{3,2,1,0:T(1,128)S(1)}, f32[2,4,1,514]{3,2,1,0:T(1,128)S(1)}, u32[]{:S(2)}, u32[]{:S(2)}) collective-permute-start(f32[2,4,1,514]{3,2,1,0:T(1,128)S(1)} %get-tuple-element.12), channel_id=1, source_target_pairs={{0,2},{2,4},{4,6},{6,8},{8,10},{10,12},{12,14},{1,3},{3,5},{5,7},{... | collective-permute-start | bytes 49352 | tf_op jit(solution)/shard_map/ppermute | solution.py:22
  81.7 31.5 %all-reduce.2.cloned.1.call-done = f32[4,64,512]{2,1,0:T(8,128)} async-done(((f32[4,64,512]{2,1,0:T(8,128)}), f32[4,64,512]{2,1,0:T(8,128)}) %all-reduce.2.cloned.1.call-update) | async-done | bytes 524304 | tf_op jit(solution)/shard_map/psum | solution.py:112
  113.3 1.1 slice_bitcast_fusion.1
  114.8 0.8 copy-done.1
  115.6 2.2 %add_select_fusion.3 = f32[2,4,64,512]{3,2,1,0:T(8,128)S(1)} fusion(f32[2,4,64,512]{3,2,1,0:T(8,128)S(1)} %copy-done.1, f32[2,4,64,1]{3,2,1,0:T(8,128)} %collective-permute-done, f32[2,4,64,1]{3,2,1,0:T(8,128)S(1)} %collective-permute-done.1, f32[2,4,1,514]{3,2,1,0:T(1,128)S(1)} %collective-permute-done.3, f32[2,4,1,514]{3,2,1,0:T(1,128)S(1)} %collective-permute-done.2, ...), kind=kLoop, calls=%fused_computation.44 | loop fusion | flops 6553600 | bytes 4264064 | tf_op jit(solution)/shard_map/jit(_where)/select_n | solution.py:40
  118.0 3.7 %collective-permute-start.5 = (f32[2,4,64,1]{3,2,1,0:T(8,128)S(1)}, f32[2,4,64,1]{3,2,1,0:T(8,128)S(1)}, u32[]{:S(2)}, u32[]{:S(2)}) collective-permute-start(f32[2,4,64,1]{3,2,1,0:T(8,128)S(1)} %get-tuple-element.17), channel_id=1, source_target_pairs={{0,16},{16,32},{32,48},{48,64},{64,80},{80,96},{96,112},{112,128},... | collective-permute-start | bytes 6152 | tf_op jit(solution)/shard_map/ppermute | solution.py:22
  121.8 5.4 %collective-permute-start.4 = (f32[2,4,64,1]{3,2,1,0:T(8,128)S(1)}, f32[2,4,64,1]{3,2,1,0:T(8,128)S(1)}, u32[]{:S(2)}, u32[]{:S(2)}) collective-permute-start(f32[2,4,64,1]{3,2,1,0:T(8,128)S(1)} %get-tuple-element.18), channel_id=1, source_target_pairs={{16,0},{32,16},{48,32},{64,48},{80,64},{96,80},{112,96},{128,112},... | collective-permute-start | bytes 6152 | tf_op jit(solution)/shard_map/ppermute | solution.py:24
  127.2 4.7 %collective-permute-done.5 = f32[2,4,64,1]{3,2,1,0:T(8,128)S(1)} collective-permute-done((f32[2,4,64,1]{3,2,1,0:T(8,128)S(1)}, f32[2,4,64,1]{3,2,1,0:T(8,128)S(1)}, u32[]{:S(2)}, u32[]{:S(2)}) %collective-permute-start.5) | collective-permute-done | bytes 2080 | tf_op jit(solution)/shard_map/ppermute | solution.py:22
  131.9 1.2 collective-permute-done.4
  133.2 2.4 %collective-permute-start.6 = (f32[2,4,1,514]{3,2,1,0:T(1,128)S(1)}, f32[2,4,1,514]{3,2,1,0:T(1,128)S(1)}, u32[]{:S(2)}, u32[]{:S(2)}) collective-permute-start(f32[2,4,1,514]{3,2,1,0:T(1,128)S(1)} %get-tuple-element.9), channel_id=1, source_target_pairs={{2,0},{4,2},{6,4},{8,6},{10,8},{12,10},{14,12},{3,1},{5,3},{7,5},{... | collective-permute-start | bytes 49352 | tf_op jit(solution)/shard_map/ppermute | solution.py:24
  135.7 3.4 %collective-permute-start.7 = (f32[2,4,1,514]{3,2,1,0:T(1,128)S(1)}, f32[2,4,1,514]{3,2,1,0:T(1,128)S(1)}, u32[]{:S(2)}, u32[]{:S(2)}) collective-permute-start(f32[2,4,1,514]{3,2,1,0:T(1,128)S(1)} %get-tuple-element.10), channel_id=1, source_target_pairs={{0,2},{2,4},{4,6},{6,8},{8,10},{10,12},{12,14},{1,3},{3,5},{5,7},{... | collective-permute-start | bytes 49352 | tf_op jit(solution)/shard_map/ppermute | solution.py:22
  139.1 3.5 %collective-permute-done.7 = f32[2,4,1,514]{3,2,1,0:T(1,128)S(1)} collective-permute-done((f32[2,4,1,514]{3,2,1,0:T(1,128)S(1)}, f32[2,4,1,514]{3,2,1,0:T(1,128)S(1)}, u32[]{:S(2)}, u32[]{:S(2)}) %collective-permute-start.7) | collective-permute-done | bytes 16480 | tf_op jit(solution)/shard_map/ppermute | solution.py:22
  142.6 1.3 add_select_fusion.2
  144.0 2.6 %collective-permute-start.9 = (f32[2,4,64,1]{3,2,1,0:T(8,128)S(1)}, f32[2,4,64,1]{3,2,1,0:T(8,128)S(1)}, u32[]{:S(2)}, u32[]{:S(2)}) collective-permute-start(f32[2,4,64,1]{3,2,1,0:T(8,128)S(1)} %get-tuple-element.15), channel_id=1, source_target_pairs={{0,16},{16,32},{32,48},{48,64},{64,80},{80,96},{96,112},{112,128},... | collective-permute-start | bytes 6152 | tf_op jit(solution)/shard_map/ppermute | solution.py:22
  146.6 7.0 %collective-permute-start.8 = (f32[2,4,64,1]{3,2,1,0:T(8,128)S(1)}, f32[2,4,64,1]{3,2,1,0:T(8,128)S(1)}, u32[]{:S(2)}, u32[]{:S(2)}) collective-permute-start(f32[2,4,64,1]{3,2,1,0:T(8,128)S(1)} %get-tuple-element.16), channel_id=1, source_target_pairs={{16,0},{32,16},{48,32},{64,48},{80,64},{96,80},{112,96},{128,112},... | collective-permute-start | bytes 6152 | tf_op jit(solution)/shard_map/ppermute | solution.py:24
  153.7 2.5 %collective-permute-done.9 = f32[2,4,64,1]{3,2,1,0:T(8,128)S(1)} collective-permute-done((f32[2,4,64,1]{3,2,1,0:T(8,128)S(1)}, f32[2,4,64,1]{3,2,1,0:T(8,128)S(1)}, u32[]{:S(2)}, u32[]{:S(2)}) %collective-permute-start.9) | collective-permute-done | bytes 2080 | tf_op jit(solution)/shard_map/ppermute | solution.py:22
  156.1 1.4 collective-permute-done.8
  157.7 1.9 collective-permute-start.10
  159.6 3.9 %collective-permute-start.11 = (f32[2,4,1,514]{3,2,1,0:T(1,128)S(1)}, f32[2,4,1,514]{3,2,1,0:T(1,128)S(1)}, u32[]{:S(2)}, u32[]{:S(2)}) collective-permute-start(f32[2,4,1,514]{3,2,1,0:T(1,128)S(1)} %get-tuple-element.8), channel_id=1, source_target_pairs={{0,2},{2,4},{4,6},{6,8},{8,10},{10,12},{12,14},{1,3},{3,5},{5,7},{... | collective-permute-start | bytes 49352 | tf_op jit(solution)/shard_map/ppermute | solution.py:22
  163.6 2.9 %collective-permute-done.11 = f32[2,4,1,514]{3,2,1,0:T(1,128)S(1)} collective-permute-done((f32[2,4,1,514]{3,2,1,0:T(1,128)S(1)}, f32[2,4,1,514]{3,2,1,0:T(1,128)S(1)}, u32[]{:S(2)}, u32[]{:S(2)}) %collective-permute-start.11) | collective-permute-done | bytes 16480 | tf_op jit(solution)/shard_map/ppermute | solution.py:22
  166.5 1.3 add_select_fusion.1
  167.9 3.3 %collective-permute-start.13 = (f32[2,4,64,1]{3,2,1,0:T(8,128)S(1)}, f32[2,4,64,1]{3,2,1,0:T(8,128)S(1)}, u32[]{:S(2)}, u32[]{:S(2)}) collective-permute-start(f32[2,4,64,1]{3,2,1,0:T(8,128)S(1)} %get-tuple-element.13), channel_id=1, source_target_pairs={{0,16},{16,32},{32,48},{48,64},{64,80},{80,96},{96,112},{112,128},... | collective-permute-start | bytes 6152 | tf_op jit(solution)/shard_map/ppermute | solution.py:22
  171.2 6.4 %collective-permute-start.12 = (f32[2,4,64,1]{3,2,1,0:T(8,128)S(1)}, f32[2,4,64,1]{3,2,1,0:T(8,128)S(1)}, u32[]{:S(2)}, u32[]{:S(2)}) collective-permute-start(f32[2,4,64,1]{3,2,1,0:T(8,128)S(1)} %get-tuple-element.14), channel_id=1, source_target_pairs={{16,0},{32,16},{48,32},{64,48},{80,64},{96,80},{112,96},{128,112},... | collective-permute-start | bytes 6152 | tf_op jit(solution)/shard_map/ppermute | solution.py:24
  177.6 2.4 %collective-permute-done.13 = f32[2,4,64,1]{3,2,1,0:T(8,128)S(1)} collective-permute-done((f32[2,4,64,1]{3,2,1,0:T(8,128)S(1)}, f32[2,4,64,1]{3,2,1,0:T(8,128)S(1)}, u32[]{:S(2)}, u32[]{:S(2)}) %collective-permute-start.13) | collective-permute-done | bytes 2080 | tf_op jit(solution)/shard_map/ppermute | solution.py:22
  180.0 1.5 collective-permute-done.12
  181.6 1.9 collective-permute-start.14
  183.6 3.9 %collective-permute-start.15 = (f32[2,4,1,514]{3,2,1,0:T(1,128)S(1)}, f32[2,4,1,514]{3,2,1,0:T(1,128)S(1)}, u32[]{:S(2)}, u32[]{:S(2)}) collective-permute-start(f32[2,4,1,514]{3,2,1,0:T(1,128)S(1)} %get-tuple-element.6), channel_id=1, source_target_pairs={{0,2},{2,4},{4,6},{6,8},{8,10},{10,12},{12,14},{1,3},{3,5},{5,7},{... | collective-permute-start | bytes 49352 | tf_op jit(solution)/shard_map/ppermute | solution.py:22
  187.5 2.9 %collective-permute-done.15 = f32[2,4,1,514]{3,2,1,0:T(1,128)S(1)} collective-permute-done((f32[2,4,1,514]{3,2,1,0:T(1,128)S(1)}, f32[2,4,1,514]{3,2,1,0:T(1,128)S(1)}, u32[]{:S(2)}, u32[]{:S(2)}) %collective-permute-start.15) | collective-permute-done | bytes 16480 | tf_op jit(solution)/shard_map/ppermute | solution.py:22
  190.5 2.2 %add_select_fusion = f32[2,4,64,512]{3,2,1,0:T(8,128)} fusion(f32[2,4,64,512]{3,2,1,0:T(8,128)S(1)} %add_select_fusion.1, f32[2,4,64,1]{3,2,1,0:T(8,128)S(1)} %collective-permute-done.12, f32[2,4,64,1]{3,2,1,0:T(8,128)S(1)} %collective-permute-done.13, f32[2,4,1,514]{3,2,1,0:T(1,128)S(1)} %collective-permute-done.15, ...), kind=kLoop, calls=%fused_computation.41 | loop fusion | flops 6553600 | bytes 4264064 | tf_op jit(solution)/shard_map/jit(_where)/select_n | solution.py:40
  (37 shorter events, 3.1 us)
Async XLA Ops:
  6.5 64.0 %copy-start = (bf16[24,128,512]{2,1,0:T(8,128)(2,1)S(1)}, bf16[24,128,512]{2,1,0:T(8,128)(2,1)}, u32[]{:S(2)}) copy-start(bf16[24,128,512]{2,1,0:T(8,128)(2,1)} %param.13) | copy-start | bytes 9437188
  9.8 29.9 %all-to-all-start = ((s32[64,1,3]{2,1,0:T(1,128)}), s32[64,1,3]{2,1,0:T(1,128)S(1)}, u32[]{:S(2)}, u32[]{:S(2)}) async-start(s32[64,1,3]{2,1,0:T(1,128)} %bitcast), calls=%async_computation | async-start | bytes 65536 | tf_op jit(solution)/shard_map/all_to_all | solution.py:106
  39.7 22.6 %all-to-all-start.1 = ((bf16[64,3,512]{2,1,0:T(4,128)(2,1)}), bf16[64,3,512]{2,1,0:T(4,128)(2,1)}, u32[]{:S(2)}, u32[]{:S(2)}) async-start(bf16[64,3,512]{2,1,0:T(4,128)(2,1)} %reshape.77), calls=%async_computation.1 | async-start | bytes 524288 | tf_op jit(solution)/shard_map/all_to_all | solution.py:99
  49.9 63.4 %all-reduce.2.cloned.1.call-start = ((), (), s32[]{:S(2)}) async-start(), calls=%async_computation.2 | async-start | bytes 1048576 | tf_op jit(solution)/shard_map/psum | solution.py:112
  51.8 22.9 %collective-permute-start.1 = (f32[2,4,64,1]{3,2,1,0:T(8,128)}, f32[2,4,64,1]{3,2,1,0:T(8,128)S(1)}, u32[]{:S(2)}, u32[]{:S(2)}) collective-permute-start(f32[2,4,64,1]{3,2,1,0:T(8,128)} %get-tuple-element.19), channel_id=1, source_target_pairs={{0,16},{16,32},{32,48},{48,64},{64,80},{80,96},{96,112},{112,128},... | collective-permute-start | bytes 6152 | tf_op jit(solution)/shard_map/ppermute | solution.py:22
  55.2 19.5 %collective-permute-start = (f32[2,4,64,1]{3,2,1,0:T(8,128)}, f32[2,4,64,1]{3,2,1,0:T(8,128)}, u32[]{:S(2)}, u32[]{:S(2)}) collective-permute-start(f32[2,4,64,1]{3,2,1,0:T(8,128)} %get-tuple-element.20), channel_id=1, source_target_pairs={{16,0},{32,16},{48,32},{64,48},{80,64},{96,80},{112,96},{128,112},... | collective-permute-start | bytes 6152 | tf_op jit(solution)/shard_map/ppermute | solution.py:24
  70.5 4.2 %copy-start.2 = (f32[3,4]{1,0:T(4,128)S(1)}, f32[3,4]{1,0:T(4,128)}, u32[]{:S(2)}) copy-start(f32[3,4]{1,0:T(4,128)} %param.15) | copy-start | bytes 148
  75.9 38.9 %collective-permute-start.2 = (f32[2,4,1,514]{3,2,1,0:T(1,128)S(1)}, f32[2,4,1,514]{3,2,1,0:T(1,128)S(1)}, u32[]{:S(2)}, u32[]{:S(2)}) collective-permute-start(f32[2,4,1,514]{3,2,1,0:T(1,128)S(1)} %get-tuple-element.11), channel_id=1, source_target_pairs={{2,0},{4,2},{6,4},{8,6},{10,8},{12,10},{14,12},{3,1},{5,3},{7,5},{... | collective-permute-start | bytes 49352 | tf_op jit(solution)/shard_map/ppermute | solution.py:24
  78.1 36.7 %collective-permute-start.3 = (f32[2,4,1,514]{3,2,1,0:T(1,128)S(1)}, f32[2,4,1,514]{3,2,1,0:T(1,128)S(1)}, u32[]{:S(2)}, u32[]{:S(2)}) collective-permute-start(f32[2,4,1,514]{3,2,1,0:T(1,128)S(1)} %get-tuple-element.12), channel_id=1, source_target_pairs={{0,2},{2,4},{4,6},{6,8},{8,10},{10,12},{12,14},{1,3},{3,5},{5,7},{... | collective-permute-start | bytes 49352 | tf_op jit(solution)/shard_map/ppermute | solution.py:22
  114.4 1.2 copy-start.1
  118.0 13.9 %collective-permute-start.5 = (f32[2,4,64,1]{3,2,1,0:T(8,128)S(1)}, f32[2,4,64,1]{3,2,1,0:T(8,128)S(1)}, u32[]{:S(2)}, u32[]{:S(2)}) collective-permute-start(f32[2,4,64,1]{3,2,1,0:T(8,128)S(1)} %get-tuple-element.17), channel_id=1, source_target_pairs={{0,16},{16,32},{32,48},{48,64},{64,80},{80,96},{96,112},{112,128},... | collective-permute-start | bytes 6152 | tf_op jit(solution)/shard_map/ppermute | solution.py:22
  121.8 11.3 %collective-permute-start.4 = (f32[2,4,64,1]{3,2,1,0:T(8,128)S(1)}, f32[2,4,64,1]{3,2,1,0:T(8,128)S(1)}, u32[]{:S(2)}, u32[]{:S(2)}) collective-permute-start(f32[2,4,64,1]{3,2,1,0:T(8,128)S(1)} %get-tuple-element.18), channel_id=1, source_target_pairs={{16,0},{32,16},{48,32},{64,48},{80,64},{96,80},{112,96},{128,112},... | collective-permute-start | bytes 6152 | tf_op jit(solution)/shard_map/ppermute | solution.py:24
  133.2 5.9 %collective-permute-start.6 = (f32[2,4,1,514]{3,2,1,0:T(1,128)S(1)}, f32[2,4,1,514]{3,2,1,0:T(1,128)S(1)}, u32[]{:S(2)}, u32[]{:S(2)}) collective-permute-start(f32[2,4,1,514]{3,2,1,0:T(1,128)S(1)} %get-tuple-element.9), channel_id=1, source_target_pairs={{2,0},{4,2},{6,4},{8,6},{10,8},{12,10},{14,12},{3,1},{5,3},{7,5},{... | collective-permute-start | bytes 49352 | tf_op jit(solution)/shard_map/ppermute | solution.py:24
  135.7 6.9 %collective-permute-start.7 = (f32[2,4,1,514]{3,2,1,0:T(1,128)S(1)}, f32[2,4,1,514]{3,2,1,0:T(1,128)S(1)}, u32[]{:S(2)}, u32[]{:S(2)}) collective-permute-start(f32[2,4,1,514]{3,2,1,0:T(1,128)S(1)} %get-tuple-element.10), channel_id=1, source_target_pairs={{0,2},{2,4},{4,6},{6,8},{8,10},{10,12},{12,14},{1,3},{3,5},{5,7},{... | collective-permute-start | bytes 49352 | tf_op jit(solution)/shard_map/ppermute | solution.py:22
  144.0 12.1 %collective-permute-start.9 = (f32[2,4,64,1]{3,2,1,0:T(8,128)S(1)}, f32[2,4,64,1]{3,2,1,0:T(8,128)S(1)}, u32[]{:S(2)}, u32[]{:S(2)}) collective-permute-start(f32[2,4,64,1]{3,2,1,0:T(8,128)S(1)} %get-tuple-element.15), channel_id=1, source_target_pairs={{0,16},{16,32},{32,48},{48,64},{64,80},{80,96},{96,112},{112,128},... | collective-permute-start | bytes 6152 | tf_op jit(solution)/shard_map/ppermute | solution.py:22
  146.6 10.9 %collective-permute-start.8 = (f32[2,4,64,1]{3,2,1,0:T(8,128)S(1)}, f32[2,4,64,1]{3,2,1,0:T(8,128)S(1)}, u32[]{:S(2)}, u32[]{:S(2)}) collective-permute-start(f32[2,4,64,1]{3,2,1,0:T(8,128)S(1)} %get-tuple-element.16), channel_id=1, source_target_pairs={{16,0},{32,16},{48,32},{64,48},{80,64},{96,80},{112,96},{128,112},... | collective-permute-start | bytes 6152 | tf_op jit(solution)/shard_map/ppermute | solution.py:24
  157.7 5.9 %collective-permute-start.10 = (f32[2,4,1,514]{3,2,1,0:T(1,128)S(1)}, f32[2,4,1,514]{3,2,1,0:T(1,128)S(1)}, u32[]{:S(2)}, u32[]{:S(2)}) collective-permute-start(f32[2,4,1,514]{3,2,1,0:T(1,128)S(1)} %get-tuple-element.7), channel_id=1, source_target_pairs={{2,0},{4,2},{6,4},{8,6},{10,8},{12,10},{14,12},{3,1},{5,3},{7,5},{... | collective-permute-start | bytes 49352 | tf_op jit(solution)/shard_map/ppermute | solution.py:24
  159.6 6.9 %collective-permute-start.11 = (f32[2,4,1,514]{3,2,1,0:T(1,128)S(1)}, f32[2,4,1,514]{3,2,1,0:T(1,128)S(1)}, u32[]{:S(2)}, u32[]{:S(2)}) collective-permute-start(f32[2,4,1,514]{3,2,1,0:T(1,128)S(1)} %get-tuple-element.8), channel_id=1, source_target_pairs={{0,2},{2,4},{4,6},{6,8},{8,10},{10,12},{12,14},{1,3},{3,5},{5,7},{... | collective-permute-start | bytes 49352 | tf_op jit(solution)/shard_map/ppermute | solution.py:22
  167.9 12.1 %collective-permute-start.13 = (f32[2,4,64,1]{3,2,1,0:T(8,128)S(1)}, f32[2,4,64,1]{3,2,1,0:T(8,128)S(1)}, u32[]{:S(2)}, u32[]{:S(2)}) collective-permute-start(f32[2,4,64,1]{3,2,1,0:T(8,128)S(1)} %get-tuple-element.13), channel_id=1, source_target_pairs={{0,16},{16,32},{32,48},{48,64},{64,80},{80,96},{96,112},{112,128},... | collective-permute-start | bytes 6152 | tf_op jit(solution)/shard_map/ppermute | solution.py:22
  171.2 10.2 %collective-permute-start.12 = (f32[2,4,64,1]{3,2,1,0:T(8,128)S(1)}, f32[2,4,64,1]{3,2,1,0:T(8,128)S(1)}, u32[]{:S(2)}, u32[]{:S(2)}) collective-permute-start(f32[2,4,64,1]{3,2,1,0:T(8,128)S(1)} %get-tuple-element.14), channel_id=1, source_target_pairs={{16,0},{32,16},{48,32},{64,48},{80,64},{96,80},{112,96},{128,112},... | collective-permute-start | bytes 6152 | tf_op jit(solution)/shard_map/ppermute | solution.py:24
  181.6 5.9 %collective-permute-start.14 = (f32[2,4,1,514]{3,2,1,0:T(1,128)S(1)}, f32[2,4,1,514]{3,2,1,0:T(1,128)S(1)}, u32[]{:S(2)}, u32[]{:S(2)}) collective-permute-start(f32[2,4,1,514]{3,2,1,0:T(1,128)S(1)} %get-tuple-element.5), channel_id=1, source_target_pairs={{2,0},{4,2},{6,4},{8,6},{10,8},{12,10},{14,12},{3,1},{5,3},{7,5},{... | collective-permute-start | bytes 49352 | tf_op jit(solution)/shard_map/ppermute | solution.py:24
  183.6 6.9 %collective-permute-start.15 = (f32[2,4,1,514]{3,2,1,0:T(1,128)S(1)}, f32[2,4,1,514]{3,2,1,0:T(1,128)S(1)}, u32[]{:S(2)}, u32[]{:S(2)}) collective-permute-start(f32[2,4,1,514]{3,2,1,0:T(1,128)S(1)} %get-tuple-element.6), channel_id=1, source_target_pairs={{0,2},{2,4},{4,6},{6,8},{8,10},{10,12},{12,14},{1,3},{3,5},{5,7},{... | collective-permute-start | bytes 49352 | tf_op jit(solution)/shard_map/ppermute | solution.py:22
Sparse Core Ops, SparseCore 0:
  73.9 39.3 all-reduce.1
where the time goes:
time: 201 us; the launch traced here: 200 us
  starting transfers between devices  93.8 us (47%)
  waiting for transfers between devices  59.8 us (30%)
  between operations  13.8 us (7%)
  other arithmetic  13.2 us (7%)
  local copies, waits for them, and re-layouts  12.6 us (6%)
  matrix products  6.25 us (3%)
    ppermute x8, starting transfers between devices, extended(): lax.ppermute(head, axis, [((i + 1) % count, i) for i in range(ends)])  33.1 us
    psum x1, waiting for transfers between devices, local(): lax.psum(remap_slots(got_flux, got_bins, remap_weights, lat_rows), 'lev')  31.5 us
    ppermute x8, starting transfers between devices, extended(): lax.ppermute(tail, axis, [(i, (i + 1) % count) for i in range(ends)])  27.8 us
    all_to_all x1, starting transfers between devices, local(): lax.all_to_all(send_bins.reshape(columns, capacity), 'col', split_axis=0,...  22.7 us
    ppermute x8, waiting for transfers between devices, extended(): lax.ppermute(tail, axis, [(i, (i + 1) % count) for i in range(ends)])  18.9 us
    all_to_all x1, starting transfers between devices, local(): lax.all_to_all(send_flux.reshape(columns, capacity, 4 * cells), 'col', sp...  10.1 us
    select_n x4, other arithmetic, advance(): return jnp.where(wet, fresh, tracer)  7.03 us
    all_to_all x1, waiting for transfers between devices, local(): lax.all_to_all(send_bins.reshape(columns, capacity), 'col', split_axis=0,...  5.3 us
  transfers between devices with their start and end apart: 19, of which 11 were waited for; matrix products, arithmetic and copies ran while one was open for 10% of the time, Pallas kernels for 0%

commit v1 on v0

v1 whole, which is shorter than its diff:
```python
import functools

import jax
import jax.numpy as jnp
from jax import lax
from jax.experimental import pallas as pl
from jax.experimental.pallas import tpu as pltpu
from jax.sharding import PartitionSpec as P

STEPS = 4
DIFFUSE = 0.2
SPEED = 0.3
FORCE_STEP = 0.25

MESH = pl.DeviceIdType.MESH
F32 = jnp.float32
BF16 = jnp.bfloat16
I32 = jnp.int32

CAP = 3
FIELDS = 4
SLOT = 64
ROWS = 64
WIDTH = 512
LANES = 128
BLOCKS = WIDTH // LANES
PAD = 8
EXT = ROWS + 2 * PAD
GROUP = EXT // 16
TILES = EXT * 8
HALO = STEPS


def row_of(ref, xb, r):
    return ref[xb, pl.ds(pl.multiple_of(r * 8, 8), 8), :]


def kernel(
    sizes,
    prof_ref,
    dest_ref,
    widx_ref,
    trow_ref,
    flux_ref,
    mask_ref,
    state_ref,
    weights_ref,
    out_ref,
    send,
    got,
    stage,
    wv,
    lhs,
    hot,
    slots,
    mine,
    theirs,
    nat,
    cells,
    force,
    coef,
    own,
    other,
    load_sem,
    out_sem,
    a2a_send,
    a2a_recv,
    lev_send,
    lev_recv,
    row_send,
    row_recv,
    col_send,
    col_recv,
):
    columns, bands = sizes
    col = lax.axis_index("col")
    row = lax.axis_index("row")
    lev = lax.axis_index("lev")
    west = lax.rem(col + columns - 1, columns)
    east = lax.rem(col + 1, columns)
    south = lax.rem(row + bands - 1, bands)
    north = lax.rem(row + 1, bands)

    state_copy = pltpu.make_async_copy(state_ref, nat, load_sem.at[0])
    weights_copy = pltpu.make_async_copy(weights_ref, wv, load_sem.at[1])
    state_copy.start()
    weights_copy.start()

    barrier = pltpu.get_barrier_semaphore()

    def greet(d, carry):
        pl.semaphore_signal(
            barrier, inc=1, device_id={"col": lax.rem(col + d, columns)}, device_id_type=MESH
        )
        return carry

    lax.fori_loop(1, columns, greet, 0)
    pl.semaphore_signal(barrier, inc=1, device_id={"row": south}, device_id_type=MESH)
    pl.semaphore_signal(barrier, inc=1, device_id={"row": north}, device_id_type=MESH)
    pl.semaphore_signal(barrier, inc=1, device_id={"lev": 1 - lev}, device_id_type=MESH)

    blocks = dest_ref.shape[1]
    dest = dest_ref[...]
    to = lax.broadcasted_iota(I32, (columns, blocks), 0)
    first = dest[0:1, :] == to
    second = dest[1:2, :] == to
    named = (first | second).astype(F32)
    before = (
        lax.broadcasted_iota(I32, (blocks, blocks), 0)
        < lax.broadcasted_iota(I32, (blocks, blocks), 1)
    ).astype(F32)
    rank = jnp.dot(named.astype(BF16), before.astype(BF16), preferred_element_type=F32)
    y_one = jnp.where(first, trow_ref[0:1, :], trow_ref[1:2, :]).astype(F32) + 1.0
    w_val = jnp.where(first, widx_ref[0:1, :], widx_ref[1:2, :]).astype(F32)
    spot = lax.broadcasted_iota(I32, (blocks, LANES), 1)
    at_y = (spot == col).astype(BF16)
    at_w = (spot == col + SLOT).astype(BF16)
    flux = flux_ref[...]
    for k in range(CAP):
        pick = jnp.where(rank == float(k), named, 0.0)
        moved = jnp.dot(pick.astype(BF16), flux, preferred_element_type=F32)
        for f in range(FIELDS):
            stage[pl.ds(k * FIELDS + f, columns, stride=16), :] = moved[:, f * LANES : (f + 1) * LANES]
        tags = jnp.dot((pick * y_one).astype(BF16), at_y, preferred_element_type=F32) + jnp.dot(
            (pick * w_val).astype(BF16), at_w, preferred_element_type=F32
        )
        stage[pl.ds(CAP * FIELDS + k, columns, stride=16), :] = tags
    stage[pl.ds(15, columns, stride=16), :] = jnp.zeros((columns, LANES), F32)
    send[...] = stage[...].astype(BF16).reshape(columns, 16, LANES)

    pl.semaphore_wait(barrier, columns + 2)

    def push(d, carry):
        target = lax.rem(col + d, columns)
        pltpu.make_async_remote_copy(
            src_ref=send.at[target],
            dst_ref=got.at[col],
            send_sem=a2a_send,
            recv_sem=a2a_recv,
            device_id={"col": target},
            device_id_type=MESH,
        ).start()
        return carry

    lax.fori_loop(1, columns, push, 0)
    got[pl.ds(col, 1)] = send[pl.ds(col, 1)]

    zero_rows = jnp.zeros((BLOCKS, PAD * 8, LANES), F32)
    spare = (PAD - HALO) * 8
    for ref in (cells.at[0], force):
        ref[:, 0:spare, :] = zero_rows[:, :spare]
        ref[:, TILES - spare : TILES, :] = zero_rows[:, :spare]
    state_copy.wait()
    for xb in range(BLOCKS):
        for t in range(8):
            cells[0, xb, pl.ds(PAD * 8 + t, ROWS, stride=8), :] = nat[t, :, xb * LANES : (xb + 1) * LANES]

    def row_copies(ref, tag, count):
        rows = count * 8
        to_north = pltpu.make_async_remote_copy(
            src_ref=ref.at[:, pl.ds((PAD + ROWS) * 8 - rows, rows), :],
            dst_ref=ref.at[:, pl.ds(PAD * 8 - rows, rows), :],
            send_sem=row_send.at[2 * tag],
            recv_sem=row_recv.at[2 * tag],
            device_id={"row": north},
            device_id_type=MESH,
        )
        to_south = pltpu.make_async_remote_copy(
            src_ref=ref.at[:, pl.ds(PAD * 8, rows), :],
            dst_ref=ref.at[:, pl.ds((PAD + ROWS) * 8, rows), :],
            send_sem=row_send.at[2 * tag + 1],
            recv_sem=row_recv.at[2 * tag + 1],
            device_id={"row": south},
            device_id_type=MESH,
        )
        return to_north, to_south

    def settle_rows(ref, copies):
        for copy in copies:
            copy.wait()

        @pl.when(row == 0)
        def _():
            ref[:, 0 : PAD * 8, :] = zero_rows

        @pl.when(row == bands - 1)
        def _():
            ref[:, (PAD + ROWS) * 8 : TILES, :] = zero_rows

    group = lax.broadcasted_iota(I32, (8, LANES), 1) // 8

    def pack(ref, tag):
        def one(j, carry):
            left = row_of(ref, 0, j)
            right = pltpu.roll(row_of(ref, BLOCKS - 1, j), 8, 1)
            for g in range(1, 16):
                r = g * GROUP + j
                left = jnp.where(group == g, pltpu.roll(row_of(ref, 0, r), 8 * g, 1), left)
                turned = row_of(ref, BLOCKS - 1, r)
                if g < 15:
                    turned = pltpu.roll(turned, 8 * g + 8, 1)
                right = jnp.where(group == g, turned, right)
            own[tag, 0, j] = left
            own[tag, 1, j] = right
            return carry

        lax.fori_loop(0, GROUP, one, 0)

    def col_copies(tag):
        to_west = pltpu.make_async_remote_copy(
            src_ref=own.at[tag, 0],
            dst_ref=other.at[tag, 1],
            send_sem=col_send.at[2 * tag],
            recv_sem=col_recv.at[2 * tag],
            device_id={"col": west},
            device_id_type=MESH,
        )
        to_east = pltpu.make_async_remote_copy(
            src_ref=own.at[tag, 1],
            dst_ref=other.at[tag, 0],
            send_sem=col_send.at[2 * tag + 1],
            recv_sem=col_recv.at[2 * tag + 1],
            device_id={"col": east},
            device_id_type=MESH,
        )
        return to_west, to_east

    def settle_cols(tag, copies):
        for copy in copies:
            copy.wait()

        @pl.when(col == 0)
        def _():
            other[tag, 0] = jnp.zeros((GROUP, 8, LANES), F32)

        @pl.when(col == columns - 1)
        def _():
            other[tag, 1] = jnp.zeros((GROUP, 8, LANES), F32)

    state_rows = row_copies(cells.at[0], 0, HALO)
    for copy in state_rows:
        copy.start()
    settle_rows(cells.at[0], state_rows)
    pack(cells.at[0], 0)
    state_cols = col_copies(0)
    for copy in state_cols:
        copy.start()
    settle_cols(0, state_cols)

    everyone = pltpu.make_async_remote_copy(
        src_ref=send.at[pl.ds(0, columns - 1)],
        dst_ref=got.at[pl.ds(0, columns - 1)],
        send_sem=a2a_send,
        recv_sem=a2a_recv,
        device_id={"col": east},
        device_id_type=MESH,
    )
    everyone.wait_recv()
    stage[...] = got[...].reshape(columns * 16, LANES).astype(F32)
    lane = lax.broadcasted_iota(I32, (1, LANES), 1)
    slots[...] = jnp.zeros_like(slots)
    bins = []
    for k in range(CAP):
        for f in range(FIELDS):
            slots[k * SLOT : k * SLOT + columns, f * LANES : (f + 1) * LANES] = stage[
                pl.ds(k * FIELDS + f, columns, stride=16), :
            ].astype(BF16)
        tags = jnp.sum(stage[pl.ds(CAP * FIELDS + k, columns, stride=16), :], axis=0, keepdims=True)
        y = tags.astype(I32) - 1
        w = pltpu.roll(tags, SLOT, 1).astype(I32)
        bins.append(jnp.where((y >= 0) & (lane < SLOT), w * ROWS + y, -1))
    low = jnp.where(lane < SLOT, bins[0], pltpu.roll(bins[1], SLOT, 1))
    bin_row = jnp.concatenate([low, bins[2]], axis=1)
    kinds = lhs.shape[1] // LANES
    batch = kinds * ROWS // 3
    for part in range(3):
        index = lax.broadcasted_iota(I32, (batch, 2 * LANES), 0) + part * batch
        hot[...] = jnp.where(index == bin_row, 1.0, 0.0).astype(BF16)
        summed = jnp.dot(hot[...], slots[...], preferred_element_type=F32).astype(BF16)
        for i in range(batch // ROWS):
            w = part * (batch // ROWS) + i
            for f in range(FIELDS):
                lhs[f * ROWS : (f + 1) * ROWS, w * LANES : (w + 1) * LANES] = summed[
                    i * ROWS : (i + 1) * ROWS, f * LANES : (f + 1) * LANES
                ]
    weights_copy.wait()
    swaps = []
    for half in range(2):
        mine[half] = jnp.dot(
            lhs[...], wv[:, half * 256 : (half + 1) * 256], preferred_element_type=F32
        )
        swap = pltpu.make_async_remote_copy(
            src_ref=mine.at[half],
            dst_ref=theirs.at[half],
            send_sem=lev_send.at[half],
            recv_sem=lev_recv.at[half],
            device_id={"lev": 1 - lev},
            device_id_type=MESH,
        )
        swap.start()
        swaps.append(swap)

    for half in range(2):
        swaps[half].wait()
        for inner in range(2):
            xb = 2 * half + inner
            here = slice(inner * LANES, (inner + 1) * LANES)
            wet = mask_ref[:, xb * LANES : (xb + 1) * LANES] == 1
            total = [
                mine[half, f * ROWS : (f + 1) * ROWS, here]
                + theirs[half, f * ROWS : (f + 1) * ROWS, here]
                for f in range(FIELDS)
            ]
            terms = [
                FORCE_STEP * total[0],
                FORCE_STEP * total[1],
                (0.5 * SPEED) * jnp.tanh(total[2]),
                (0.5 * SPEED) * jnp.tanh(total[3]),
                jnp.full((ROWS, LANES), DIFFUSE, F32),
            ]
            for f, term in enumerate(terms):
                force[xb, pl.ds(PAD * 8 + f, ROWS, stride=8), :] = jnp.where(wet, term, 0.0)
            for f in range(len(terms), 8):
                force[xb, pl.ds(PAD * 8 + f, ROWS, stride=8), :] = jnp.zeros((ROWS, LANES), F32)
    force_rows = row_copies(force, 1, HALO)
    for copy in force_rows:
        copy.start()

    tracer = lax.broadcasted_iota(I32, (8, LANES), 0)

    def profile(index, keep):
        value = jnp.zeros((8, LANES), F32)
        for level in range(4):
            value = jnp.where(
                (lax.rem(tracer, 4) == level) & keep, prof_ref[index, level], value
            )
        return value

    heat = profile(0, tracer < 4)
    fresh = profile(1, tracer >= 4)
    decay = profile(2, tracer >= 0)

    def factors(term):
        spread = [jnp.broadcast_to(term(f), (8, LANES)) for f in range(5)]
        source = spread[0] * heat + spread[1] * fresh
        a = spread[2] * decay
        b = spread[3] * decay
        d = spread[4]
        return 1.0 - 4.0 * d, d - a, d + a, d - b, d + b, source

    lanes = lax.broadcasted_iota(I32, (8, LANES), 1)

    def sides(cur):
        back = [pltpu.roll(c, 1, 1) for c in cur]
        ahead = [pltpu.roll(c, LANES - 1, 1) for c in cur]
        from_west = [jnp.where(lanes == 0, back[xb - 1], back[xb]) for xb in range(BLOCKS)]
        from_east = [
            jnp.where(lanes == LANES - 1, ahead[(xb + 1) % BLOCKS], ahead[xb])
            for xb in range(BLOCKS)
        ]
        return from_west, from_east

    def combine(c, below, cur, above, left, right):
        return (
            (c[0] * cur + c[5]) + (c[1] * right + c[2] * left) + (c[3] * above + c[4] * below)
        )

    def advance_row(step, r, below, cur, make):
        above = [row_of(cells.at[step], xb, r + 1) for xb in range(BLOCKS)]
        left, right = sides(cur)
        at = pl.ds(pl.multiple_of(r * 8, 8), 8)
        for xb in range(BLOCKS):
            if make:
                c = factors(lambda f: force[xb, pl.ds(r * 8 + f, 1), :])
                for i in range(6):
                    coef[i, xb, at, :] = c[i]
            else:
                c = [coef[i, xb, at, :] for i in range(6)]
            cells[step + 1, xb, at, :] = combine(c, below[xb], cur[xb], above[xb], left[xb], right[xb])
        return cur, above

    def sweep(step, low_row, count, make, unroll):
        below = [row_of(cells.at[step], xb, low_row - 1) for xb in range(BLOCKS)]
        cur = [row_of(cells.at[step], xb, low_row) for xb in range(BLOCKS)]

        def body(i, carry):
            below, cur = list(carry[:BLOCKS]), list(carry[BLOCKS:])
            for u in range(unroll):
                below, cur = advance_row(step, low_row + i * unroll + u, below, cur, make)
            return (*below, *cur)

        lax.fori_loop(0, count // unroll, body, (*below, *cur))

    sweep(0, PAD, ROWS, True, 2)
    settle_rows(force, force_rows)
    pack(force, 1)
    force_cols = col_copies(1)
    for copy in force_cols:
        copy.start()
    for step in range(1, STEPS):
        sweep(step, PAD + step, ROWS - 2 * step, False, 2)
    for step in range(STEPS):
        reach = STEPS - 1 - step
        for base in (PAD - reach, PAD + ROWS - step):
            below = [row_of(cells.at[step], xb, base - 1) for xb in range(BLOCKS)]
            cur = [row_of(cells.at[step], xb, base) for xb in range(BLOCKS)]
            for r in range(base, base + STEPS - 1):
                below, cur = advance_row(step, r, below, cur, step == 0)
    settle_cols(1, force_cols)

    spot8 = lax.rem(lax.broadcasted_iota(I32, (GROUP, 8, LANES), 2), 8)

    def strip_factors(ref):
        parts = [factors(lambda f: ref[j, f : f + 1, :]) for j in range(GROUP)]
        return [jnp.stack([p[i] for p in parts]) for i in range(6)]

    def turn(x, shift):
        return pltpu.roll(x, shift % LANES, 2)

    def strip(lefts, rights):
        (l_cells, l_force), (r_cells, r_force) = lefts, rights
        pair = [l_cells[...], r_cells[...]]
        cs = [strip_factors(l_force), strip_factors(r_force)]
        for _ in range(STEPS):
            rolled = []
            for side in range(2):
                x = pair[side]
                above = jnp.concatenate([x[1:], turn(x[:1], -8)], axis=0)
                below = jnp.concatenate([turn(x[-1:], 8), x[:-1]], axis=0)
                right, left = turn(x, -1), turn(x, 1)
                if side == 0:
                    right = jnp.where(spot8 == 7, turn(pair[1], 7), right)
                else:
                    left = jnp.where(spot8 == 0, turn(pair[0], -7), left)
                rolled.append(combine(cs[side], below, x, above, left, right))
            pair = rolled
        return pair

    own[0, 0] = strip((other.at[0, 0], other.at[1, 0]), (own.at[0, 0], own.at[1, 0]))[1]
    own[0, 1] = strip((own.at[0, 1], own.at[1, 1]), (other.at[0, 1], other.at[1, 1]))[0]
    last = cells.at[STEPS]
    for r in range(PAD, PAD + ROWS):
        g, j = r // GROUP, r % GROUP
        at = pl.ds(r * 8, 8)
        last[0, at, :] = jnp.where(lanes < 4, pltpu.roll(own[0, 0, j], (LANES - 8 * g) % LANES, 1), last[0, at, :])
        last[BLOCKS - 1, at, :] = jnp.where(
            lanes >= LANES - 4,
            pltpu.roll(own[0, 1, j], (LANES - 8 - 8 * g) % LANES, 1),
            last[BLOCKS - 1, at, :],
        )
    for t in range(8):
        for xb in range(BLOCKS):
            nat[t, :, xb * LANES : (xb + 1) * LANES] = last[xb, pl.ds(PAD * 8 + t, ROWS, stride=8), :]
    result = pltpu.make_async_copy(nat, out_ref, out_sem)
    result.start()
    result.wait()
    everyone.wait_send()


def local(
    state, atm_flux, intersection, weight_index, target_row, remap_weights, land_mask, profiles
):
    columns, bands = lax.axis_size("col"), lax.axis_size("row")
    per_device = atm_flux.shape[2]
    kinds, cells, width = remap_weights.shape

    def lists(x):
        return x.reshape(per_device, 2).T

    vmem = pl.BlockSpec(memory_space=pltpu.VMEM)
    hbm = pl.BlockSpec(memory_space=pl.ANY)
    dma = pltpu.SemaphoreType.DMA
    out = pl.pallas_call(
        functools.partial(kernel, (columns, bands)),
        out_shape=jax.ShapeDtypeStruct((8, ROWS, WIDTH), F32),
        in_specs=[pl.BlockSpec(memory_space=pltpu.SMEM)] + [vmem] * 5 + [hbm] * 2,
        out_specs=hbm,
        scratch_shapes=[
            pltpu.VMEM((columns, 16, LANES), BF16),
            pltpu.VMEM((columns, 16, LANES), BF16),
            pltpu.VMEM((columns * 16, LANES), F32),
            pltpu.VMEM((kinds * cells, width), BF16),
            pltpu.VMEM((FIELDS * ROWS, kinds * cells), BF16),
            pltpu.VMEM((kinds * ROWS // 3, 2 * LANES), BF16),
            pltpu.VMEM((2 * LANES, FIELDS * cells), BF16),
            pltpu.VMEM((2, FIELDS * ROWS, width // 2), F32),
            pltpu.VMEM((2, FIELDS * ROWS, width // 2), F32),
            pltpu.VMEM((8, ROWS, WIDTH), F32),
            pltpu.VMEM((STEPS + 1, BLOCKS, TILES, LANES), F32),
            pltpu.VMEM((BLOCKS, TILES, LANES), F32),
            pltpu.VMEM((6, BLOCKS, TILES, LANES), F32),
            pltpu.VMEM((2, 2, GROUP, 8, LANES), F32),
            pltpu.VMEM((2, 2, GROUP, 8, LANES), F32),
            dma((2,)),
            dma,
            dma,
            dma,
            dma((2,)),
            dma((2,)),
            dma((4,)),
            dma((4,)),
            dma((4,)),
            dma((4,)),
        ],
        compiler_params=pltpu.CompilerParams(
            collective_id=0, has_side_effects=True, vmem_limit_bytes=48 * 1024 * 1024
        ),
    )(
        profiles,
        lists(intersection),
        lists(weight_index),
        lists(target_row),
        atm_flux.reshape(per_device, FIELDS * cells),
        land_mask,
        state.reshape(8, ROWS, WIDTH),
        remap_weights.reshape(kinds * cells, width),
    )
    return out.reshape(state.shape)


def solution(mesh):
    in_specs = (
        P(None, "lev", "row", "col"),
        P("row", "lev", "col", None),
        P("row", "lev", "col", None),
        P("row", "lev", "col", None),
        P("row", "lev", "col", None),
        P(),
        P("row", "col"),
        P(None, "lev"),
    )
    out_specs = P(None, "lev", "row", "col")
    return jax.shard_map(local, mesh=mesh, in_specs=in_specs, out_specs=out_specs, check_vma=False)
```

time: 201 us -> 62.3 us (0.31)
  the two profiles are of different devices: /device:TPU:72 before, /device:TPU:1 now
where the time goes in v1:
time: 62.3 us; the launch traced here: 62 us
  Pallas kernels  53.5 us (86%)
  local copies, waits for them, and re-layouts  8.5 us (14%)
    pallas_call x1, Pallas kernels, local(): pl.pallas_call(functools.partial(kernel, (columns, bands)), out_shape=jax...  53.5 us
    unnamed x17, local copies, waits for them, and re-layouts  8.5 us

profile of v1, /device:TPU:1, one launch (start us, length us, event | category | flops | bytes accessed | tf_op | source)
XLA Modules:
  0.0 62.0 jit_solution(5609230515302635539)
XLA Ops:
  0.0 0.0 copy-start
  0.0 1.9 %copy-done = bf16[24,128,512]{2,1,0:T(8,128)(2,1)S(1)} copy-done((bf16[24,128,512]{2,1,0:T(8,128)(2,1)S(1)}, bf16[24,128,512]{2,1,0:T(8,128)(2,1)}, u32[]{:S(2)}) %copy-start) | copy-done | bytes 3145752
  1.9 0.0 copy-start.1
  1.9 1.2 %copy-done.1 = f32[2,4,64,512]{3,2,1,0:T(8,128)S(1)} copy-done((f32[2,4,64,512]{3,2,1,0:T(8,128)S(1)}, f32[2,4,64,512]{3,2,1,0:T(8,128)}, u32[]{:S(2)}) %copy-start.1) | copy-done | bytes 1048600
  3.1 0.0 copy-start.2
  3.1 0.9 %copy-done.2 = s32[64,512]{1,0:T(8,128)S(1)} copy-done((s32[64,512]{1,0:T(8,128)S(1)}, s32[64,512]{1,0:T(8,128)}, u32[]{:S(2)}) %copy-start.2) | copy-done | bytes 131096
  4.0 0.0 copy-start.3
  4.0 0.8 %copy-done.3 = bf16[1,1,48,512]{3,2,1,0:T(8,128)(2,1)S(1)} copy-done((bf16[1,1,48,512]{3,2,1,0:T(8,128)(2,1)S(1)}, bf16[1,1,48,512]{3,2,1,0:T(8,128)(2,1)}, u32[]{:S(2)}) %copy-start.3) | copy-done | bytes 49176
  4.8 0.0 copy-start.4
  4.8 0.7 %copy-done.4 = f32[3,4]{1,0:T(4,128)S(1)} copy-done((f32[3,4]{1,0:T(4,128)S(1)}, f32[3,4]{1,0:T(4,128)}, u32[]{:S(2)}) %copy-start.4) | copy-done | bytes 72
  5.5 0.0 copy-start.5
  5.5 0.7 %copy-done.5 = s32[1,1,48,2]{2,3,1,0:T(2,128)S(1)} copy-done((s32[1,1,48,2]{2,3,1,0:T(2,128)S(1)}, s32[1,1,48,2]{2,3,1,0:T(2,128)}, u32[]{:S(2)}) %copy-start.5) | copy-done | bytes 408
  6.2 0.0 copy-start.6
  6.2 0.7 %copy-done.6 = s32[1,1,48,2]{2,3,1,0:T(2,128)S(1)} copy-done((s32[1,1,48,2]{2,3,1,0:T(2,128)S(1)}, s32[1,1,48,2]{2,3,1,0:T(2,128)}, u32[]{:S(2)}) %copy-start.6) | copy-done | bytes 408
  6.9 0.0 copy-start.7
  6.9 0.7 %copy-done.7 = s32[1,1,48,2]{2,3,1,0:T(2,128)S(1)} copy-done((s32[1,1,48,2]{2,3,1,0:T(2,128)S(1)}, s32[1,1,48,2]{2,3,1,0:T(2,128)}, u32[]{:S(2)}) %copy-start.7) | copy-done | bytes 408
  7.5 53.5 %shard_map.82 = f32[8,64,512]{2,1,0:T(8,128)S(1)} custom-call(f32[3,4]{1,0:T(4,128)S(1)} %copy-done.4, s32[2,48]{1,0:T(2,128)S(1)} %bitcast.17, s32[2,48]{1,0:T(2,128)S(1)} %bitcast.18, s32[2,48]{1,0:T(2,128)S(1)} %bitcast.19, bf16[48,512]{1,0:T(8,128)(2,1)S(1)} %bitcast.16, s32[64,512]{1,0:T(8,128)S(1)} %copy-done.2, f32[8,64,512]{2,1,0:T(8,128)S(1)} %bitcast.15, ...), custom_call_target="tpu_custom_call" | custom-call | tf_op jit(solution)/shard_map/pallas_call | solution.py:473
  61.0 1.0 %copy.10 = f32[2,4,64,512]{3,2,1,0:T(8,128)} copy(f32[2,4,64,512]{3,2,1,0:T(8,128)S(1)} %bitcast.13) | data formatting | bytes 2097152
Async XLA Ops:
  0.0 1.9 %copy-start = (bf16[24,128,512]{2,1,0:T(8,128)(2,1)S(1)}, bf16[24,128,512]{2,1,0:T(8,128)(2,1)}, u32[]{:S(2)}) copy-start(bf16[24,128,512]{2,1,0:T(8,128)(2,1)} %param.13) | copy-start | bytes 9437188
  1.9 1.2 %copy-start.1 = (f32[2,4,64,512]{3,2,1,0:T(8,128)S(1)}, f32[2,4,64,512]{3,2,1,0:T(8,128)}, u32[]{:S(2)}) copy-start(f32[2,4,64,512]{3,2,1,0:T(8,128)} %param.8) | copy-start | bytes 3145732
  3.1 0.9 %copy-start.2 = (s32[64,512]{1,0:T(8,128)S(1)}, s32[64,512]{1,0:T(8,128)}, u32[]{:S(2)}) copy-start(s32[64,512]{1,0:T(8,128)} %mask_ref.1) | copy-start | bytes 393220
  4.0 0.8 %copy-start.3 = (bf16[1,1,48,512]{3,2,1,0:T(8,128)(2,1)S(1)}, bf16[1,1,48,512]{3,2,1,0:T(8,128)(2,1)}, u32[]{:S(2)}) copy-start(bf16[1,1,48,512]{3,2,1,0:T(8,128)(2,1)} %param.9) | copy-start | bytes 147460
  4.8 0.7 %copy-start.4 = (f32[3,4]{1,0:T(4,128)S(1)}, f32[3,4]{1,0:T(4,128)}, u32[]{:S(2)}) copy-start(f32[3,4]{1,0:T(4,128)} %prof_ref.1) | copy-start | bytes 148
  5.5 0.7 %copy-start.5 = (s32[1,1,48,2]{2,3,1,0:T(2,128)S(1)}, s32[1,1,48,2]{2,3,1,0:T(2,128)}, u32[]{:S(2)}) copy-start(s32[1,1,48,2]{2,3,1,0:T(2,128)} %param.10) | copy-start | bytes 1156
  6.2 0.7 %copy-start.6 = (s32[1,1,48,2]{2,3,1,0:T(2,128)S(1)}, s32[1,1,48,2]{2,3,1,0:T(2,128)}, u32[]{:S(2)}) copy-start(s32[1,1,48,2]{2,3,1,0:T(2,128)} %param.11) | copy-start | bytes 1156
  6.9 0.7 %copy-start.7 = (s32[1,1,48,2]{2,3,1,0:T(2,128)S(1)}, s32[1,1,48,2]{2,3,1,0:T(2,128)}, u32[]{:S(2)}) copy-start(s32[1,1,48,2]{2,3,1,0:T(2,128)} %param.12) | copy-start | bytes 1156

commit v2 on v1

--- a/solution.py
+++ b/solution.py
@@ -1,4 +1,5 @@
 import functools
+import math
 
 import jax
 import jax.numpy as jnp
@@ -32,20 +33,39 @@
 
 
 def row_of(ref, xb, r):
-    return ref[xb, pl.ds(pl.multiple_of(r * 8, 8), 8), :]
+    if not isinstance(r, int):
+        r = pl.multiple_of(r * 8, 8)
+    else:
+        r = r * 8
+    return ref[xb, pl.ds(r, 8), :]
+
+
+def far_first(col, columns):
+    side = math.isqrt(columns)
+
+    def hops(offset):
+        return sum(min(part, side - part) for part in divmod(offset, side))
+
+    return [
+        lax.rem(col // side + offset // side, side) * side + lax.rem(col % side + offset % side, side)
+        for offset in sorted(range(1, columns), key=lambda offset: (-hops(offset), -offset))
+    ]
 
 
 def kernel(
     sizes,
     prof_ref,
-    dest_ref,
-    widx_ref,
-    trow_ref,
-    flux_ref,
-    mask_ref,
+    dest_hbm,
+    widx_hbm,
+    trow_hbm,
+    flux_hbm,
+    mask_hbm,
     state_ref,
     weights_ref,
     out_ref,
+    pairs,
+    flux_ref,
+    mask_ref,
     send,
     got,
     stage,
@@ -83,24 +103,29 @@
 
     state_copy = pltpu.make_async_copy(state_ref, nat, load_sem.at[0])
     weights_copy = pltpu.make_async_copy(weights_ref, wv, load_sem.at[1])
-    state_copy.start()
-    weights_copy.start()
+    pair_copies = [
+        pltpu.make_async_copy(ref, pairs.at[i], load_sem.at[2 + i])
+        for i, ref in enumerate((dest_hbm, widx_hbm, trow_hbm))
+    ]
+    flux_copy = pltpu.make_async_copy(flux_hbm, flux_ref, load_sem.at[5])
+    mask_copy = pltpu.make_async_copy(mask_hbm, mask_ref, load_sem.at[6])
+    for copy in pair_copies + [flux_copy, state_copy, weights_copy, mask_copy]:
+        copy.start()
 
     barrier = pltpu.get_barrier_semaphore()
 
-    def greet(d, carry):
-        pl.semaphore_signal(
-            barrier, inc=1, device_id={"col": lax.rem(col + d, columns)}, device_id_type=MESH
-        )
-        return carry
-
-    lax.fori_loop(1, columns, greet, 0)
+    peers = far_first(col, columns)
+    for peer in peers:
+        pl.semaphore_signal(barrier, inc=1, device_id={"col": peer}, device_id_type=MESH)
     pl.semaphore_signal(barrier, inc=1, device_id={"row": south}, device_id_type=MESH)
     pl.semaphore_signal(barrier, inc=1, device_id={"row": north}, device_id_type=MESH)
     pl.semaphore_signal(barrier, inc=1, device_id={"lev": 1 - lev}, device_id_type=MESH)
 
-    blocks = dest_ref.shape[1]
-    dest = dest_ref[...]
+    for copy in pair_copies:
+        copy.wait()
+    flux_copy.wait()
+    blocks = pairs.shape[2]
+    dest, kind, goal = pairs[0], pairs[1], pairs[2]
     to = lax.broadcasted_iota(I32, (columns, blocks), 0)
     first = dest[0:1, :] == to
     second = dest[1:2, :] == to
@@ -110,8 +135,8 @@
         < lax.broadcasted_iota(I32, (blocks, blocks), 1)
     ).astype(F32)
     rank = jnp.dot(named.astype(BF16), before.astype(BF16), preferred_element_type=F32)
-    y_one = jnp.where(first, trow_ref[0:1, :], trow_ref[1:2, :]).astype(F32) + 1.0
-    w_val = jnp.where(first, widx_ref[0:1, :], widx_ref[1:2, :]).astype(F32)
+    y_one = jnp.where(first, goal[0:1, :], goal[1:2, :]).astype(F32) + 1.0
+    w_val = jnp.where(first, kind[0:1, :], kind[1:2, :]).astype(F32)
     spot = lax.broadcasted_iota(I32, (blocks, LANES), 1)
     at_y = (spot == col).astype(BF16)
     at_w = (spot == col + SLOT).astype(BF16)
@@ -130,30 +155,27 @@
 
     pl.semaphore_wait(barrier, columns + 2)
 
-    def push(d, carry):
-        target = lax.rem(col + d, columns)
+    for peer in peers:
         pltpu.make_async_remote_copy(
-            src_ref=send.at[target],
+            src_ref=send.at[peer],
             dst_ref=got.at[col],
             send_sem=a2a_send,
             recv_sem=a2a_recv,
-            device_id={"col": target},
+            device_id={"col": peer},
             device_id_type=MESH,
         ).start()
-        return carry
-
-    lax.fori_loop(1, columns, push, 0)
     got[pl.ds(col, 1)] = send[pl.ds(col, 1)]
 
     zero_rows = jnp.zeros((BLOCKS, PAD * 8, LANES), F32)
     spare = (PAD - HALO) * 8
-    for ref in (cells.at[0], force):
+    for ref in (cells[0], force):
         ref[:, 0:spare, :] = zero_rows[:, :spare]
         ref[:, TILES - spare : TILES, :] = zero_rows[:, :spare]
+    force[:, PAD * 8 : (PAD + ROWS) * 8, :] = jnp.zeros((BLOCKS, ROWS * 8, LANES), F32)
     state_copy.wait()
     for xb in range(BLOCKS):
         for t in range(8):
-            cells[0, xb, pl.ds(PAD * 8 + t, ROWS, stride=8), :] = nat[t, :, xb * LANES : (xb + 1) * LANES]
+            cells[0][xb, pl.ds(PAD * 8 + t, ROWS, stride=8), :] = nat[t, :, xb * LANES : (xb + 1) * LANES]
 
     def row_copies(ref, tag, count):
         rows = count * 8
@@ -237,11 +259,11 @@
         def _():
             other[tag, 1] = jnp.zeros((GROUP, 8, LANES), F32)
 
-    state_rows = row_copies(cells.at[0], 0, HALO)
+    state_rows = row_copies(cells[0], 0, HALO)
     for copy in state_rows:
         copy.start()
-    settle_rows(cells.at[0], state_rows)
-    pack(cells.at[0], 0)
+    settle_rows(cells[0], state_rows)
+    pack(cells[0], 0)
     state_cols = col_copies(0)
     for copy in state_cols:
         copy.start()
@@ -285,21 +307,27 @@
                 ]
     weights_copy.wait()
     swaps = []
-    for half in range(2):
-        mine[half] = jnp.dot(
-            lhs[...], wv[:, half * 256 : (half + 1) * 256], preferred_element_type=F32
-        )
-        swap = pltpu.make_async_remote_copy(
-            src_ref=mine.at[half],
-            dst_ref=theirs.at[half],
+
+    def swap(source, target, half):
+        return pltpu.make_async_remote_copy(
+            src_ref=source,
+            dst_ref=target,
             send_sem=lev_send.at[half],
             recv_sem=lev_recv.at[half],
             device_id={"lev": 1 - lev},
             device_id_type=MESH,
         )
-        swap.start()
-        swaps.append(swap)
-
+
+    for half in range(2):
+        mine[half] = jnp.dot(
+            lhs[...], wv[:, half * 256 : (half + 1) * 256], preferred_element_type=F32
+        )
+        for f in range(FIELDS):
+            part = pl.ds(f * ROWS, ROWS)
+            swap(mine.at[half, part], theirs.at[half, part], half).start()
+        swaps.append(swap(mine.at[half], theirs.at[half], half))
+
+    mask_copy.wait()
     for half in range(2):
         swaps[half].wait()
         for inner in range(2):
@@ -320,8 +348,6 @@
             ]
             for f, term in enumerate(terms):
                 force[xb, pl.ds(PAD * 8 + f, ROWS, stride=8), :] = jnp.where(wet, term, 0.0)
-            for f in range(len(terms), 8):
-                force[xb, pl.ds(PAD * 8 + f, ROWS, stride=8), :] = jnp.zeros((ROWS, LANES), F32)
     force_rows = row_copies(force, 1, HALO)
     for copy in force_rows:
         copy.start()
@@ -365,47 +391,55 @@
             (c[0] * cur + c[5]) + (c[1] * right + c[2] * left) + (c[3] * above + c[4] * below)
         )
 
-    def advance_row(step, r, below, cur, make):
-        above = [row_of(cells.at[step], xb, r + 1) for xb in range(BLOCKS)]
-        left, right = sides(cur)
-        at = pl.ds(pl.multiple_of(r * 8, 8), 8)
-        for xb in range(BLOCKS):
-            if make:
-                c = factors(lambda f: force[xb, pl.ds(r * 8 + f, 1), :])
-                for i in range(6):
-                    coef[i, xb, at, :] = c[i]
-            else:
-                c = [coef[i, xb, at, :] for i in range(6)]
-            cells[step + 1, xb, at, :] = combine(c, below[xb], cur[xb], above[xb], left[xb], right[xb])
-        return cur, above
-
-    def sweep(step, low_row, count, make, unroll):
-        below = [row_of(cells.at[step], xb, low_row - 1) for xb in range(BLOCKS)]
-        cur = [row_of(cells.at[step], xb, low_row) for xb in range(BLOCKS)]
-
-        def body(i, carry):
-            below, cur = list(carry[:BLOCKS]), list(carry[BLOCKS:])
-            for u in range(unroll):
-                below, cur = advance_row(step, low_row + i * unroll + u, below, cur, make)
-            return (*below, *cur)
-
-        lax.fori_loop(0, count // unroll, body, (*below, *cur))
-
-    sweep(0, PAD, ROWS, True, 2)
+    def update_rows(step, base, count, make):
+        table = [
+            [row_of(cells[step], xb, base + q) for xb in range(BLOCKS)] for q in range(-1, count + 1)
+        ]
+        results = []
+        for q in range(count):
+            below, cur, above = table[q : q + 3]
+            left, right = sides(cur)
+            at = pl.ds((base + q) * 8, 8)
+            for xb in range(BLOCKS):
+                if make:
+                    c = factors(lambda f: force[xb, pl.ds((base + q) * 8 + f, 1), :])
+                    for i in range(6):
+                        coef[i, xb, at, :] = c[i]
+                else:
+                    c = [coef[i, xb, at, :] for i in range(6)]
+                results.append(
+                    (xb, at, combine(c, below[xb], cur[xb], above[xb], left[xb], right[xb]))
+                )
+        for xb, at, value in results:
+            cells[step + 1][xb, at, :] = value
+
+    def sweep(step, low_row, count, make):
+        for start in range(0, count, 4):
+            update_rows(step, low_row + start, min(4, count - start), make)
+
+    sweep(0, PAD, ROWS, True)
     settle_rows(force, force_rows)
     pack(force, 1)
     force_cols = col_copies(1)
     for copy in force_cols:
         copy.start()
     for step in range(1, STEPS):
-        sweep(step, PAD + step, ROWS - 2 * step, False, 2)
+        sweep(step, PAD + step, ROWS - 2 * step, False)
     for step in range(STEPS):
-        reach = STEPS - 1 - step
-        for base in (PAD - reach, PAD + ROWS - step):
-            below = [row_of(cells.at[step], xb, base - 1) for xb in range(BLOCKS)]
-            cur = [row_of(cells.at[step], xb, base) for xb in range(BLOCKS)]
-            for r in range(base, base + STEPS - 1):
-                below, cur = advance_row(step, r, below, cur, step == 0)
+        for base in (PAD - (STEPS - 1 - step), PAD + ROWS - step):
+            update_rows(step, base, STEPS - 1, step == 0)
+    last = cells[STEPS]
+
+    def results(low, high, sem):
+        for t in range(8):
+            for xb in range(low, high):
+                nat[t, :, xb * LANES : (xb + 1) * LANES] = last[xb, pl.ds(PAD * 8 + t, ROWS, stride=8), :]
+        part = pl.ds(low * LANES, (high - low) * LANES)
+        copy = pltpu.make_async_copy(nat.at[:, :, part], out_ref.at[:, :, part], sem)
+        copy.start()
+        return copy
+
+    inner = results(1, BLOCKS - 1, out_sem.at[0])
     settle_cols(1, force_cols)
 
     spot8 = lax.rem(lax.broadcasted_iota(I32, (GROUP, 8, LANES), 2), 8)
@@ -438,7 +472,6 @@
 
     own[0, 0] = strip((other.at[0, 0], other.at[1, 0]), (own.at[0, 0], own.at[1, 0]))[1]
     own[0, 1] = strip((own.at[0, 1], own.at[1, 1]), (other.at[0, 1], other.at[1, 1]))[0]
-    last = cells.at[STEPS]
     for r in range(PAD, PAD + ROWS):
         g, j = r // GROUP, r % GROUP
         at = pl.ds(r * 8, 8)
@@ -448,12 +481,9 @@
             pltpu.roll(own[0, 1, j], (LANES - 8 - 8 * g) % LANES, 1),
             last[BLOCKS - 1, at, :],
         )
-    for t in range(8):
-        for xb in range(BLOCKS):
-            nat[t, :, xb * LANES : (xb + 1) * LANES] = last[xb, pl.ds(PAD * 8 + t, ROWS, stride=8), :]
-    result = pltpu.make_async_copy(nat, out_ref, out_sem)
-    result.start()
-    result.wait()
+    outer = [results(0, 1, out_sem.at[1]), results(BLOCKS - 1, BLOCKS, out_sem.at[2])]
+    for copy in [inner] + outer:
+        copy.wait()
     everyone.wait_send()
 
 
@@ -467,15 +497,17 @@
     def lists(x):
         return x.reshape(per_device, 2).T
 
-    vmem = pl.BlockSpec(memory_space=pltpu.VMEM)
     hbm = pl.BlockSpec(memory_space=pl.ANY)
     dma = pltpu.SemaphoreType.DMA
     out = pl.pallas_call(
         functools.partial(kernel, (columns, bands)),
         out_shape=jax.ShapeDtypeStruct((8, ROWS, WIDTH), F32),
-        in_specs=[pl.BlockSpec(memory_space=pltpu.SMEM)] + [vmem] * 5 + [hbm] * 2,
+        in_specs=[pl.BlockSpec(memory_space=pltpu.SMEM)] + [hbm] * 7,
         out_specs=hbm,
         scratch_shapes=[
+            pltpu.VMEM((3, 2, per_device), I32),
+            pltpu.VMEM((per_device, FIELDS * cells), BF16),
+            pltpu.VMEM((ROWS, WIDTH), I32),
             pltpu.VMEM((columns, 16, LANES), BF16),
             pltpu.VMEM((columns, 16, LANES), BF16),
             pltpu.VMEM((columns * 16, LANES), F32),
@@ -486,13 +518,13 @@
             pltpu.VMEM((2, FIELDS * ROWS, width // 2), F32),
             pltpu.VMEM((2, FIELDS * ROWS, width // 2), F32),
             pltpu.VMEM((8, ROWS, WIDTH), F32),
-            pltpu.VMEM((STEPS + 1, BLOCKS, TILES, LANES), F32),
+            [pltpu.VMEM((BLOCKS, TILES, LANES), F32)] * (STEPS + 1),
             pltpu.VMEM((BLOCKS, TILES, LANES), F32),
             pltpu.VMEM((6, BLOCKS, TILES, LANES), F32),
             pltpu.VMEM((2, 2, GROUP, 8, LANES), F32),
             pltpu.VMEM((2, 2, GROUP, 8, LANES), F32),
-            dma((2,)),
-            dma,
+            dma((7,)),
+            dma((3,)),
             dma,
             dma,
             dma((2,)),
@@ -503,7 +535,7 @@
             dma((4,)),
         ],
         compiler_params=pltpu.CompilerParams(
-            collective_id=0, has_side_effects=True, vmem_limit_bytes=48 * 1024 * 1024
+            collective_id=0, has_side_effects=True, vmem_limit_bytes=62 * 1024 * 1024
         ),
     )(
         profiles,

time: 62.3 us -> 51.3 us (0.82)
  local copies, waits for them, and re-layouts: 8.5 us -> 2.26 us
  Pallas kernels: 53.5 us -> 48.9 us
    unnamed x17 -> x1, local copies, waits for them, and re-layouts: 8.5 us -> 2.26 us
    pallas_call x1, Pallas kernels: 53.5 us -> 48.9 us  [local(): pl.pallas_call(functools.partial(kernel, (columns, bands)), out_shape=jax...]
where the time goes in v2:
time: 51.3 us; the launch traced here: 51.1 us
  Pallas kernels  48.9 us (95%)
  local copies, waits for them, and re-layouts  2.26 us (4%)
    pallas_call x1, Pallas kernels, local(): pl.pallas_call(functools.partial(kernel, (columns, bands)), out_shape=jax...  48.9 us
    unnamed x1, local copies, waits for them, and re-layouts  2.26 us

profile of v2, /device:TPU:1, one launch (start us, length us, event | category | flops | bytes accessed | tf_op | source)
XLA Modules:
  0.0 51.1 jit_solution(13372464774609215863)
XLA Ops:
  0.0 48.9 %shard_map.82 = f32[8,64,512]{2,1,0:T(8,128)} custom-call(f32[3,4]{1,0:T(4,128)} %prof_ref.1, s32[2,48]{1,0:T(2,128)} %bitcast.17, s32[2,48]{1,0:T(2,128)} %bitcast.18, s32[2,48]{1,0:T(2,128)} %bitcast.19, bf16[48,512]{1,0:T(8,128)(2,1)} %bitcast.16, s32[64,512]{1,0:T(8,128)} %mask_hbm.1, f32[8,64,512]{2,1,0:T(8,128)} %bitcast.15, bf16[3072,512]{1,0:T(8,128)(2,1)} %bitcast.14), custom_call_target="tpu_custom_call" | custom-call | tf_op jit(solution)/shard_map/pallas_call | solution.py:502
  48.9 2.3 %copy.10 = f32[2,4,64,512]{3,2,1,0:T(8,128)} copy(f32[2,4,64,512]{3,2,1,0:T(8,128)} %bitcast.13) | data formatting | bytes 2097152

commit v3 on v2

--- a/solution.py
+++ b/solution.py
@@ -54,7 +54,7 @@
 
 def kernel(
     sizes,
-    prof_ref,
+    prof_hbm,
     dest_hbm,
     widx_hbm,
     trow_hbm,
@@ -63,6 +63,7 @@
     state_ref,
     weights_ref,
     out_ref,
+    prof_ref,
     pairs,
     flux_ref,
     mask_ref,
@@ -74,7 +75,7 @@
     hot,
     slots,
     mine,
-    theirs,
+    twin,
     nat,
     cells,
     force,
@@ -82,7 +83,6 @@
     own,
     other,
     load_sem,
-    out_sem,
     a2a_send,
     a2a_recv,
     lev_send,
@@ -109,7 +109,8 @@
     ]
     flux_copy = pltpu.make_async_copy(flux_hbm, flux_ref, load_sem.at[5])
     mask_copy = pltpu.make_async_copy(mask_hbm, mask_ref, load_sem.at[6])
-    for copy in pair_copies + [flux_copy, state_copy, weights_copy, mask_copy]:
+    prof_copy = pltpu.make_async_copy(prof_hbm, prof_ref, load_sem.at[7])
+    for copy in pair_copies + [flux_copy, state_copy, weights_copy, mask_copy, prof_copy]:
         copy.start()
 
     barrier = pltpu.get_barrier_semaphore()
@@ -269,6 +270,7 @@
         copy.start()
     settle_cols(0, state_cols)
 
+    slots[...] = jnp.zeros_like(slots)
     everyone = pltpu.make_async_remote_copy(
         src_ref=send.at[pl.ds(0, columns - 1)],
         dst_ref=got.at[pl.ds(0, columns - 1)],
@@ -278,67 +280,66 @@
         device_id_type=MESH,
     )
     everyone.wait_recv()
-    stage[...] = got[...].reshape(columns * 16, LANES).astype(F32)
+    relay = pltpu.make_async_remote_copy(
+        src_ref=got,
+        dst_ref=twin,
+        send_sem=lev_send,
+        recv_sem=lev_recv,
+        device_id={"lev": 1 - lev},
+        device_id_type=MESH,
+    )
+    relay.start()
     lane = lax.broadcasted_iota(I32, (1, LANES), 1)
-    slots[...] = jnp.zeros_like(slots)
-    bins = []
-    for k in range(CAP):
-        for f in range(FIELDS):
-            slots[k * SLOT : k * SLOT + columns, f * LANES : (f + 1) * LANES] = stage[
-                pl.ds(k * FIELDS + f, columns, stride=16), :
-            ].astype(BF16)
-        tags = jnp.sum(stage[pl.ds(CAP * FIELDS + k, columns, stride=16), :], axis=0, keepdims=True)
-        y = tags.astype(I32) - 1
-        w = pltpu.roll(tags, SLOT, 1).astype(I32)
-        bins.append(jnp.where((y >= 0) & (lane < SLOT), w * ROWS + y, -1))
-    low = jnp.where(lane < SLOT, bins[0], pltpu.roll(bins[1], SLOT, 1))
-    bin_row = jnp.concatenate([low, bins[2]], axis=1)
     kinds = lhs.shape[1] // LANES
     batch = kinds * ROWS // 3
-    for part in range(3):
-        index = lax.broadcasted_iota(I32, (batch, 2 * LANES), 0) + part * batch
-        hot[...] = jnp.where(index == bin_row, 1.0, 0.0).astype(BF16)
-        summed = jnp.dot(hot[...], slots[...], preferred_element_type=F32).astype(BF16)
-        for i in range(batch // ROWS):
-            w = part * (batch // ROWS) + i
+
+    def group_pairs(source):
+        stage[...] = source[...].reshape(columns * 16, LANES).astype(F32)
+        bins = []
+        for k in range(CAP):
             for f in range(FIELDS):
-                lhs[f * ROWS : (f + 1) * ROWS, w * LANES : (w + 1) * LANES] = summed[
-                    i * ROWS : (i + 1) * ROWS, f * LANES : (f + 1) * LANES
-                ]
+                slots[k * SLOT : k * SLOT + columns, f * LANES : (f + 1) * LANES] = stage[
+                    pl.ds(k * FIELDS + f, columns, stride=16), :
+                ].astype(BF16)
+            tags = jnp.sum(
+                stage[pl.ds(CAP * FIELDS + k, columns, stride=16), :], axis=0, keepdims=True
+            )
+            y = tags.astype(I32) - 1
+            w = pltpu.roll(tags, SLOT, 1).astype(I32)
+            bins.append(jnp.where((y >= 0) & (lane < SLOT), w * ROWS + y, -1))
+        low = jnp.where(lane < SLOT, bins[0], pltpu.roll(bins[1], SLOT, 1))
+        bin_row = jnp.concatenate([low, bins[2]], axis=1)
+        for part in range(3):
+            index = lax.broadcasted_iota(I32, (batch, 2 * LANES), 0) + part * batch
+            hot[...] = jnp.where(index == bin_row, 1.0, 0.0).astype(BF16)
+            summed = jnp.dot(hot[...], slots[...], preferred_element_type=F32).astype(BF16)
+            for i in range(batch // ROWS):
+                w = part * (batch // ROWS) + i
+                for f in range(FIELDS):
+                    lhs[f * ROWS : (f + 1) * ROWS, w * LANES : (w + 1) * LANES] = summed[
+                        i * ROWS : (i + 1) * ROWS, f * LANES : (f + 1) * LANES
+                    ]
+
+    group_pairs(got)
     weights_copy.wait()
-    swaps = []
-
-    def swap(source, target, half):
-        return pltpu.make_async_remote_copy(
-            src_ref=source,
-            dst_ref=target,
-            send_sem=lev_send.at[half],
-            recv_sem=lev_recv.at[half],
-            device_id={"lev": 1 - lev},
-            device_id_type=MESH,
-        )
-
     for half in range(2):
         mine[half] = jnp.dot(
             lhs[...], wv[:, half * 256 : (half + 1) * 256], preferred_element_type=F32
         )
-        for f in range(FIELDS):
-            part = pl.ds(f * ROWS, ROWS)
-            swap(mine.at[half, part], theirs.at[half, part], half).start()
-        swaps.append(swap(mine.at[half], theirs.at[half], half))
-
     mask_copy.wait()
+    prof_copy.wait()
+    relay.wait()
+    group_pairs(twin)
+
     for half in range(2):
-        swaps[half].wait()
+        mine[half] += jnp.dot(
+            lhs[...], wv[:, half * 256 : (half + 1) * 256], preferred_element_type=F32
+        )
         for inner in range(2):
             xb = 2 * half + inner
             here = slice(inner * LANES, (inner + 1) * LANES)
             wet = mask_ref[:, xb * LANES : (xb + 1) * LANES] == 1
-            total = [
-                mine[half, f * ROWS : (f + 1) * ROWS, here]
-                + theirs[half, f * ROWS : (f + 1) * ROWS, here]
-                for f in range(FIELDS)
-            ]
+            total = [mine[half, f * ROWS : (f + 1) * ROWS, here] for f in range(FIELDS)]
             terms = [
                 FORCE_STEP * total[0],
                 FORCE_STEP * total[1],
@@ -430,16 +431,12 @@
             update_rows(step, base, STEPS - 1, step == 0)
     last = cells[STEPS]
 
-    def results(low, high, sem):
+    def results(xb):
         for t in range(8):
-            for xb in range(low, high):
-                nat[t, :, xb * LANES : (xb + 1) * LANES] = last[xb, pl.ds(PAD * 8 + t, ROWS, stride=8), :]
-        part = pl.ds(low * LANES, (high - low) * LANES)
-        copy = pltpu.make_async_copy(nat.at[:, :, part], out_ref.at[:, :, part], sem)
-        copy.start()
-        return copy
-
-    inner = results(1, BLOCKS - 1, out_sem.at[0])
+            out_ref[t, :, xb * LANES : (xb + 1) * LANES] = last[xb, pl.ds(PAD * 8 + t, ROWS, stride=8), :]
+
+    for xb in range(1, BLOCKS - 1):
+        results(xb)
     settle_cols(1, force_cols)
 
     spot8 = lax.rem(lax.broadcasted_iota(I32, (GROUP, 8, LANES), 2), 8)
@@ -481,9 +478,8 @@
             pltpu.roll(own[0, 1, j], (LANES - 8 - 8 * g) % LANES, 1),
             last[BLOCKS - 1, at, :],
         )
-    outer = [results(0, 1, out_sem.at[1]), results(BLOCKS - 1, BLOCKS, out_sem.at[2])]
-    for copy in [inner] + outer:
-        copy.wait()
+    results(0)
+    results(BLOCKS - 1)
     everyone.wait_send()
 
 
@@ -501,10 +497,11 @@
     dma = pltpu.SemaphoreType.DMA
     out = pl.pallas_call(
         functools.partial(kernel, (columns, bands)),
-        out_shape=jax.ShapeDtypeStruct((8, ROWS, WIDTH), F32),
-        in_specs=[pl.BlockSpec(memory_space=pltpu.SMEM)] + [hbm] * 7,
-        out_specs=hbm,
+        out_shape=pltpu.VMEM((8, ROWS, WIDTH), F32),
+        in_specs=[hbm] * 8,
+        out_specs=pl.BlockSpec(memory_space=pltpu.VMEM),
         scratch_shapes=[
+            pltpu.SMEM(profiles.shape, F32),
             pltpu.VMEM((3, 2, per_device), I32),
             pltpu.VMEM((per_device, FIELDS * cells), BF16),
             pltpu.VMEM((ROWS, WIDTH), I32),
@@ -516,36 +513,40 @@
             pltpu.VMEM((kinds * ROWS // 3, 2 * LANES), BF16),
             pltpu.VMEM((2 * LANES, FIELDS * cells), BF16),
             pltpu.VMEM((2, FIELDS * ROWS, width // 2), F32),
-            pltpu.VMEM((2, FIELDS * ROWS, width // 2), F32),
+            pltpu.VMEM((columns, 16, LANES), BF16),
             pltpu.VMEM((8, ROWS, WIDTH), F32),
             [pltpu.VMEM((BLOCKS, TILES, LANES), F32)] * (STEPS + 1),
             pltpu.VMEM((BLOCKS, TILES, LANES), F32),
             pltpu.VMEM((6, BLOCKS, TILES, LANES), F32),
             pltpu.VMEM((2, 2, GROUP, 8, LANES), F32),
             pltpu.VMEM((2, 2, GROUP, 8, LANES), F32),
-            dma((7,)),
-            dma((3,)),
+            dma((8,)),
             dma,
             dma,
-            dma((2,)),
-            dma((2,)),
+            dma,
+            dma,
             dma((4,)),
             dma((4,)),
             dma((4,)),
             dma((4,)),
         ],
         compiler_params=pltpu.CompilerParams(
-            collective_id=0, has_side_effects=True, vmem_limit_bytes=62 * 1024 * 1024
+            collective_id=0, has_side_effects=True, vmem_limit_bytes=48 * 1024 * 1024
         ),
     )(
-        profiles,
-        lists(intersection),
-        lists(weight_index),
-        lists(target_row),
-        atm_flux.reshape(per_device, FIELDS * cells),
-        land_mask,
-        state.reshape(8, ROWS, WIDTH),
-        remap_weights.reshape(kinds * cells, width),
+        *(
+            pltpu.with_memory_space_constraint(x, pltpu.HBM)
+            for x in (
+                profiles,
+                lists(intersection),
+                lists(weight_index),
+                lists(target_row),
+                atm_flux.reshape(per_device, FIELDS * cells),
+                land_mask,
+                state.reshape(8, ROWS, WIDTH),
+                remap_weights.reshape(kinds * cells, width),
+            )
+        ),
     )
     return out.reshape(state.shape)
 

time: 51.3 us -> 47.4 us (0.924); the launches traced: 51.1 us -> 46.5 us
  Pallas kernels: 48.9 us -> 45.6 us
  local copies, waits for them, and re-layouts: 2.26 us -> 0.97 us
    pallas_call x1, Pallas kernels: 48.9 us -> 45.6 us  [local(): pl.pallas_call(functools.partial(kernel, (columns, bands)), out_shape=plt...]
    unnamed x1, local copies, waits for them, and re-layouts: 2.26 us -> 0.97 us
where the time goes in v3:
time: 47.4 us; the launch traced here: 46.5 us
  Pallas kernels  45.6 us (96%)
  local copies, waits for them, and re-layouts  0.97 us (2%)
    pallas_call x1, Pallas kernels, local(): pl.pallas_call(functools.partial(kernel, (columns, bands)), out_shape=plt...  45.6 us
    unnamed x1, local copies, waits for them, and re-layouts  0.97 us

profile of v3, /device:TPU:1, one launch (start us, length us, event | category | flops | bytes accessed | tf_op | source)
XLA Modules:
  0.0 46.5 jit_solution(6936226504803507927)
XLA Ops:
  0.0 45.6 %shard_map.82 = f32[8,64,512]{2,1,0:T(8,128)S(1)} custom-call(f32[3,4]{1,0:T(4,128)} %prof_hbm.1, s32[2,48]{1,0:T(2,128)} %bitcast.17, s32[2,48]{1,0:T(2,128)} %bitcast.18, s32[2,48]{1,0:T(2,128)} %bitcast.19, bf16[48,512]{1,0:T(8,128)(2,1)} %bitcast.16, s32[64,512]{1,0:T(8,128)} %mask_hbm.1, f32[8,64,512]{2,1,0:T(8,128)} %bitcast.15, bf16[3072,512]{1,0:T(8,128)(2,1)} %bitcast.14), custom_call_target="tpu_custom_call" | custom-call | tf_op jit(solution)/shard_map/pallas_call | solution.py:498
  45.6 1.0 %copy.10 = f32[2,4,64,512]{3,2,1,0:T(8,128)} copy(f32[2,4,64,512]{3,2,1,0:T(8,128)S(1)} %bitcast.13) | data formatting | bytes 2097152

commit v4 on v3

--- a/solution.py
+++ b/solution.py
@@ -40,14 +40,15 @@
     return ref[xb, pl.ds(r, 8), :]
 
 
-def far_first(col, columns):
+def far_first(col, lev, columns):
     side = math.isqrt(columns)
 
     def hops(offset):
         return sum(min(part, side - part) for part in divmod(offset, side))
 
+    x, z, way = col // side + side, col % side + side, 1 - 2 * lev
     return [
-        lax.rem(col // side + offset // side, side) * side + lax.rem(col % side + offset % side, side)
+        lax.rem(x + way * (offset // side), side) * side + lax.rem(z + way * (offset % side), side)
         for offset in sorted(range(1, columns), key=lambda offset: (-hops(offset), -offset))
     ]
 
@@ -110,17 +111,19 @@
     flux_copy = pltpu.make_async_copy(flux_hbm, flux_ref, load_sem.at[5])
     mask_copy = pltpu.make_async_copy(mask_hbm, mask_ref, load_sem.at[6])
     prof_copy = pltpu.make_async_copy(prof_hbm, prof_ref, load_sem.at[7])
-    for copy in pair_copies + [flux_copy, state_copy, weights_copy, mask_copy, prof_copy]:
+    for copy in pair_copies + [flux_copy]:
         copy.start()
 
     barrier = pltpu.get_barrier_semaphore()
 
-    peers = far_first(col, columns)
+    peers = far_first(col, lev, columns)
     for peer in peers:
         pl.semaphore_signal(barrier, inc=1, device_id={"col": peer}, device_id_type=MESH)
     pl.semaphore_signal(barrier, inc=1, device_id={"row": south}, device_id_type=MESH)
     pl.semaphore_signal(barrier, inc=1, device_id={"row": north}, device_id_type=MESH)
     pl.semaphore_signal(barrier, inc=1, device_id={"lev": 1 - lev}, device_id_type=MESH)
+    for copy in (state_copy, weights_copy, mask_copy, prof_copy):
+        copy.start()
 
     for copy in pair_copies:
         copy.wait()
@@ -419,12 +422,13 @@
             update_rows(step, low_row + start, min(4, count - start), make)
 
     sweep(0, PAD, ROWS, True)
+    sweep(1, PAD + 1, ROWS - 2, False)
     settle_rows(force, force_rows)
     pack(force, 1)
     force_cols = col_copies(1)
     for copy in force_cols:
         copy.start()
-    for step in range(1, STEPS):
+    for step in range(2, STEPS):
         sweep(step, PAD + step, ROWS - 2 * step, False)
     for step in range(STEPS):
         for base in (PAD - (STEPS - 1 - step), PAD + ROWS - step):

time: 47.4 us -> 47.5 us (level)
  the two profiles are of different devices: /device:TPU:1 before, /device:TPU:2 now
where the time goes in v4:
time: 47.5 us; the launch traced here: 47.3 us
  Pallas kernels  46.3 us (97%)
  local copies, waits for them, and re-layouts  0.97 us (2%)
    pallas_call x1, Pallas kernels, local(): pl.pallas_call(functools.partial(kernel, (columns, bands)), out_shape=plt...  46.3 us
    unnamed x1, local copies, waits for them, and re-layouts  0.97 us

profile of v4, /device:TPU:2, one launch (start us, length us, event | category | flops | bytes accessed | tf_op | source)
XLA Modules:
  0.0 47.3 jit_solution(1357038646886616764)
XLA Ops:
  0.0 46.3 %shard_map.82 = f32[8,64,512]{2,1,0:T(8,128)S(1)} custom-call(f32[3,4]{1,0:T(4,128)} %prof_hbm.1, s32[2,48]{1,0:T(2,128)} %bitcast.17, s32[2,48]{1,0:T(2,128)} %bitcast.18, s32[2,48]{1,0:T(2,128)} %bitcast.19, bf16[48,512]{1,0:T(8,128)(2,1)} %bitcast.16, s32[64,512]{1,0:T(8,128)} %mask_hbm.1, f32[8,64,512]{2,1,0:T(8,128)} %bitcast.15, bf16[3072,512]{1,0:T(8,128)(2,1)} %bitcast.14), custom_call_target="tpu_custom_call" | custom-call | tf_op jit(solution)/shard_map/pallas_call | solution.py:502
  46.3 1.0 %copy.10 = f32[2,4,64,512]{3,2,1,0:T(8,128)} copy(f32[2,4,64,512]{3,2,1,0:T(8,128)S(1)} %bitcast.13) | data formatting | bytes 2097152
